TPU v7x, 32 devices: a whole 2x2x4 slice. The times are simulated.
32 devices in a mesh: section: 2 (over x), dp: 4 (over z), tensor: 4 (over y, core).
Axes of the slice: x: 2, y: 2, z: 4, core: 2. Of those that a mesh axis runs over, the one named last changes fastest.
Arguments:
- vision_rows: bfloat16 [1024, 12800], P(('section', 'dp')), may hold values from -100 to 100
- vision_gain: float32 [12800], replicated, may hold values from 0.1 to 1.9
- vision_bias: float32 [12800], replicated, may hold values from -4 to 4
- proj_weight: bfloat16 [12800, 4096], P(('section', 'dp'), 'tensor'), may hold values from -0.0546875 to 0.0546875
- text_rows: bfloat16 [1024, 4096], P(('section', 'dp'), 'tensor'), may hold values from -100 to 100
- text_gain: float32 [4096], P('tensor'), may hold values from 0.1 to 1.9
- slot_of_row: int32 [1024], P(('section', 'dp')), may hold values from -1 to 1023, as said below
- out_cotangent: bfloat16 [1024, 4096], P(('section', 'dp'), 'tensor'), may hold values from -6 to 6
Outputs:
- normed: bfloat16 [1024, 4096], P(('section', 'dp'), 'tensor')
- vision_grad: bfloat16 [1024, 12800], P(('section', 'dp', 'tensor'))
Inputs may be any that keep to these rules, and one draw needn't show every extreme that they name: `slot_of_row`: language device g (index g of section+dp) owns slots g * 128 to (g + 1) * 128 - 1. Rows come in aligned runs of 16: a run is all -1 or goes to 16 consecutive slots that start at a multiple of 16. A vision device sends only to language devices with the same dp index, at most 8 // 2 runs to each. No slot receives two rows. In every draw some vision device has all its runs live and some language device receives a row in every slot.
All inputs are finite; a program needn't handle non-finite values.
Results may differ from a plain program's by a relative error of at most 0.0064.
Values may be sent and summed in bfloat16 or wider, within the bound.
A program may use at most 128 MiB of HBM per device.

v0:
```python
import jax
import jax.numpy as jnp
from jax import lax
from jax.sharding import PartitionSpec as P

D = 4096
UNIT = 16


VISION_EPS = 1e-05
EPSILON = 1e-06
HALF_ROOT = 0.7071067811865476
INV_ROOT_TWO_PI = 0.3989422804014327


def gelu_value(values):
    return 0.5 * values * (1.0 + lax.erf(values * HALF_ROOT))


def gelu_slope(values):
    return (
        0.5 * (1.0 + lax.erf(values * HALF_ROOT))
        + values * jnp.exp(-0.5 * values * values) * INV_ROOT_TWO_PI
    )


def shards(
    vision_rows,
    vision_gain,
    vision_bias,
    proj_weight,
    text_rows,
    text_gain,
    slot_of_row,
    out_cotangent,
):
    sections = lax.axis_size("section")
    groups = lax.axis_size("dp")
    tensor_count = lax.axis_size("tensor")
    row_total = vision_rows.shape[0]
    lang_total = text_rows.shape[0]
    column_count = text_rows.shape[1]
    unit_total = row_total // UNIT
    lang_units = lang_total // UNIT
    capacity = unit_total // sections
    bucket_count = sections * capacity
    vision_wide = vision_rows.astype(jnp.float32)
    centered = vision_wide - jnp.mean(vision_wide, axis=1, keepdims=True)
    vision_inv = lax.rsqrt(jnp.mean(centered * centered, axis=1, keepdims=True) + VISION_EPS)
    vision_hat = centered * vision_inv
    normed_vision = (vision_hat * vision_gain + vision_bias).astype(jnp.bfloat16)
    weight_all = lax.all_gather(proj_weight, ("section", "dp"), axis=0, tiled=True)
    projected = jnp.dot(normed_vision, weight_all, preferred_element_type=jnp.float32)
    features = gelu_value(projected).astype(jnp.bfloat16)
    unit_slot = slot_of_row.reshape(unit_total, UNIT)[:, 0]
    unit_live = unit_slot >= 0
    target_device = jnp.where(unit_live, unit_slot // lang_total, 0) // groups
    same_target = (
        (target_device[:, None] == target_device[None, :]) & unit_live[:, None] & unit_live[None, :]
    )
    unit_order = jnp.arange(unit_total)
    earlier = unit_order[None, :] < unit_order[:, None]
    unit_rank = jnp.sum((same_target & earlier).astype(jnp.int32), axis=1)
    bucket = jnp.clip(target_device * capacity + unit_rank, 0, bucket_count - 1)
    chosen = (jnp.arange(bucket_count)[:, None] == bucket[None, :]) & unit_live[None, :]
    chosen_int = chosen.astype(jnp.int32)
    bucket_used = jnp.sum(chosen_int, axis=1) > 0
    bucket_source = jnp.sum(chosen_int * unit_order[None, :], axis=1)
    feature_units = features.reshape(unit_total, UNIT * column_count)
    send_rows = jnp.where(
        bucket_used[:, None], feature_units[bucket_source], jnp.zeros((), jnp.bfloat16)
    )
    send_slots = jnp.where(bucket_used, jnp.sum(chosen_int * unit_slot[None, :], axis=1), -1)
    arrived, arrived_slots = (
        lax.all_to_all(
            send_rows.reshape(sections, capacity * UNIT, column_count),
            "section",
            split_axis=0,
            concat_axis=0,
            tiled=True,
        ),
        lax.all_to_all(
            send_slots.reshape(sections, capacity),
            "section",
            split_axis=0,
            concat_axis=0,
            tiled=True,
        ),
    )
    lang_index = lax.axis_index("section") * groups + lax.axis_index("dp")
    arrived_slots = arrived_slots.reshape(bucket_count)
    arrived_live = arrived_slots >= 0
    arrived_position = jnp.clip(
        (arrived_slots - lang_index * lang_total) // UNIT, 0, lang_units - 1
    )
    placement = (jnp.arange(lang_units)[:, None] == arrived_position[None, :]) & arrived_live[
        None, :
    ]
    placement_int = placement.astype(jnp.int32)
    slot_is_image = jnp.sum(placement_int, axis=1) > 0
    slot_source = jnp.sum(placement_int * jnp.arange(bucket_count)[None, :], axis=1)
    arrived_units = arrived.reshape(bucket_count, UNIT * column_count)
    hidden_units = jnp.where(
        slot_is_image[:, None],
        arrived_units[slot_source],
        text_rows.reshape(lang_units, UNIT * column_count),
    )
    hidden_wide = hidden_units.reshape(lang_total, column_count).astype(jnp.float32)
    square_total = lax.psum(jnp.sum(hidden_wide * hidden_wide, axis=1), "tensor")
    hidden_inv = lax.rsqrt(square_total / D + EPSILON)[:, None]
    normed = (hidden_wide * hidden_inv * text_gain).astype(jnp.bfloat16)
    upstream = out_cotangent.astype(jnp.float32) * text_gain
    cross_total = lax.psum(jnp.sum(upstream * hidden_wide, axis=1), "tensor")
    cross_mean = (cross_total / D)[:, None]
    hidden_grad = (
        hidden_inv * (upstream - hidden_wide * hidden_inv * hidden_inv * cross_mean)
    ).astype(jnp.bfloat16)
    grad_units = hidden_grad.reshape(lang_units, UNIT * column_count)
    reply_rows = jnp.where(
        arrived_live[:, None], grad_units[arrived_position], jnp.zeros((), jnp.bfloat16)
    )
    returned = lax.all_to_all(
        reply_rows.reshape(sections, capacity * UNIT, column_count),
        "section",
        split_axis=0,
        concat_axis=0,
        tiled=True,
    )
    returned_units = returned.reshape(bucket_count, UNIT * column_count)
    feature_grad = jnp.where(
        unit_live[:, None], returned_units[bucket], jnp.zeros((), jnp.bfloat16)
    )
    feature_grad = feature_grad.reshape(row_total, column_count)
    projected_grad = (feature_grad.astype(jnp.float32) * gelu_slope(projected)).astype(jnp.bfloat16)
    share = row_total // tensor_count
    share_start = lax.axis_index("tensor") * share
    contract_dims = (((1,), (1,)), ((), ()))
    partial_grad = lax.dot_general(
        projected_grad, weight_all, contract_dims, preferred_element_type=jnp.float32
    )
    normed_grad = lax.psum_scatter(partial_grad, "tensor", scatter_dimension=0, tiled=True)
    own_hat = lax.dynamic_slice_in_dim(vision_hat, share_start, share, 0)
    own_inv = lax.dynamic_slice_in_dim(vision_inv, share_start, share, 0)
    weighted = normed_grad * vision_gain
    weighted_mean = jnp.mean(weighted, axis=1, keepdims=True)
    vision_cross = jnp.mean(weighted * own_hat, axis=1, keepdims=True)
    vision_grad = own_inv * (weighted - weighted_mean - own_hat * vision_cross)
    return (normed, vision_grad.astype(jnp.bfloat16))


def solution(mesh):
    in_specs = (
        P(("section", "dp"), None),
        P(),
        P(),
        P(("section", "dp"), "tensor"),
        P(("section", "dp"), "tensor"),
        P("tensor"),
        P(("section", "dp")),
        P(("section", "dp"), "tensor"),
    )
    out_specs = (P(("section", "dp"), "tensor"), P(("section", "dp", "tensor"), None))
    return jax.shard_map(shards, mesh=mesh, in_specs=in_specs, out_specs=out_specs, check_vma=False)
```

profile of v0, /device:TPU:0, one launch (start us, length us, event | category | flops | bytes accessed | tf_op | source)
XLA Modules:
  0.0 663.3 jit_solution(3732136806898014205)
XLA Ops:
  7.2 0.7 all-gather.2.cloned.1.call-update
  7.9 1.0 reshape.320
  9.6 0.6 select_n.138
  10.3 4.2 all-to-all-start
  14.7 0.6 broadcast_in_dim.90
  15.5 2.4 convert_reduce_fusion
  17.9 1.1 fusion.2
  19.5 0.7 fusion.51
  20.3 0.6 broadcast_compare_fusion
  21.3 0.6 fusion.35
  21.9 0.7 fusion.36
  22.6 0.6 broadcast_compare_fusion.1
  23.2 489.2 %all-gather.2.cloned.1.call-done = bf16[12800,1024]{1,0:T(8,128)(2,1)} async-done(((bf16[1600,1024]{1,0:T(8,128)(2,1)}), bf16[12800,1024]{1,0:T(8,128)(2,1)}) %all-gather.2.cloned.1.call-update) | async-done | bytes 26214416 | tf_op jit(solution)/shard_map/all_gather | solution.py:52
  512.4 13.1 %multiply_convert_fusion.1 = (bf16[128,1024]{1,0:T(8,128)(2,1)}, f32[128,1024]{1,0:T(8,128)}) fusion(bf16[12800,1024]{1,0:T(8,128)(2,1)} %all-gather.2.cloned.1.call-done, f32[12800]{0:T(1024)S(1)} %copy-done.9, f32[12800]{0:T(1024)S(1)} %copy-done.1, f32[128]{0:T(128)S(1)} %add_rsqrt_fusion.1, f32[128]{0:T(128)S(1)} %broadcast_multiply_fusion.3, ...), kind=kOutput, calls=%fused_computation.36 | convolution fusion | flops 3365928960 | bytes 30381056 | tf_op jit(solution)/shard_map/dot_general | solution.py:53
  525.5 1.1 reshape.321
  526.6 1.4 gather_fusion
  528.0 1.1 gather.21
  529.1 1.4 broadcast_select_fusion.2
  530.4 4.1 all-to-all-start.1
  534.6 1.2 pad_clamp_fusion.2
  535.8 0.8 broadcast_in_dim.86
  536.5 0.6 broadcast_in_dim.87
  537.1 0.7 copy.70
  537.8 0.7 broadcast_in_dim.97
  538.5 0.6 pad_clamp_fusion.1
  539.2 0.9 all-to-all-done.1
  540.1 1.1 reshape.322
  541.1 1.5 gather_fusion.1
  542.7 1.8 gather.23
  544.5 2.0 fusion.14
  546.4 6.3 all-reduce
  552.8 0.7 add_rsqrt_fusion
  553.4 2.0 fusion.12
  555.4 1.1 reshape.323
  556.5 1.4 gather_fusion.2
  557.9 1.1 gather.25
  559.0 1.5 broadcast_select_fusion.1
  560.4 4.1 all-to-all-start.2
  564.9 0.7 broadcast_in_dim.93
  565.7 4.4 all-to-all-done.2
  570.1 1.1 reshape.324
  571.2 1.4 gather_fusion.3
  572.6 1.1 gather.27
  573.7 15.9 %fusion.21 = f32[128,12800]{1,0:T(8,128)} fusion(bf16[12800,1024]{1,0:T(8,128)(2,1)} %all-gather.2.cloned.1.call-done, f32[128,1024]{1,0:T(8,128)} %get-tuple-element.26, bf16[128,1024]{1,0:T(8,128)(2,1)S(1)} %gather.27, pred[128]{0:T(512)(128)(4,1)S(1)} %broadcast_in_dim.94), kind=kOutput, calls=%fused_computation.38 | convolution fusion | flops 3357016064 | bytes 33554560 | tf_op jit(solution)/shard_map/dot_general | solution.py:138
  590.2 3.7 fusion
  593.9 57.1 %reduce-scatter.2.cloned.1.call-done = f32[32,12800]{1,0:T(8,128)} async-done(((f32[128,12800]{1,0:T(8,128)}), f32[32,12800]{1,0:T(8,128)}) %reduce-scatter.2.cloned.1.call-update) | async-done | bytes 1638416 | tf_op jit(solution)/shard_map/reduce_scatter | solution.py:141
  651.0 2.2 multiply_reduce_fusion.1
  653.2 3.2 multiply_convert_fusion
  (55 shorter events, 3.4 us)
Async XLA Ops:
  7.2 10.8 %copy-start = (bf16[128,12800]{1,0:T(8,128)(2,1)S(1)}, bf16[128,12800]{1,0:T(8,128)(2,1)}, u32[]{:S(2)}) copy-start(bf16[128,12800]{1,0:T(8,128)(2,1)} %param.8) | copy-start | bytes 9830404
  7.2 505.2 %copy-start.9 = (f32[12800]{0:T(1024)S(1)}, f32[12800]{0:T(1024)}, u32[]{:S(2)}) copy-start(f32[12800]{0:T(1024)} %param.10) | copy-start | bytes 153604
  7.2 505.2 %copy-start.1 = (f32[12800]{0:T(1024)S(1)}, f32[12800]{0:T(1024)}, u32[]{:S(2)}) copy-start(f32[12800]{0:T(1024)} %param.9) | copy-start | bytes 153604
  7.2 505.2 %all-gather.2.cloned.1.call-start = ((), (), s32[]{:S(2)}) async-start(), calls=%async_computation.4 | async-start | bytes 29491200 | tf_op jit(solution)/shard_map/all_gather | solution.py:52
  9.0 516.4 %copy-start.6 = (pred[8]{0:T(512)(128)(4,1)}, pred[8]{0:T(512)(128)(4,1)S(1)}, u32[]{:S(2)}) copy-start(pred[8]{0:T(512)(128)(4,1)S(1)} %get-tuple-element.16) | copy-start | bytes 28
  10.3 8.8 %all-to-all-start = ((s32[2,1,4]{2,1,0:T(1,128)}), s32[2,1,4]{2,1,0:T(1,128)S(1)}, u32[]{:S(2)}, u32[]{:S(2)}) async-start(s32[2,1,4]{2,1,0:T(1,128)} %bitcast), calls=%async_computation | async-start | bytes 2048 | tf_op jit(solution)/shard_map/all_to_all | solution.py:82
  17.9 507.5 %copy-start.4 = (f32[128]{0:T(128)}, f32[128]{0:T(128)S(1)}, u32[]{:S(2)}) copy-start(f32[128]{0:T(128)S(1)} %broadcast_multiply_fusion.3) | copy-start | bytes 1540
  19.0 506.5 %copy-start.7 = (f32[128]{0:T(128)}, f32[128]{0:T(128)S(1)}, u32[]{:S(2)}) copy-start(f32[128]{0:T(128)S(1)} %add_rsqrt_fusion.1) | copy-start | bytes 1540
  525.5 19.0 %copy-start.3 = (f32[1024]{0:T(1024)S(1)}, f32[1024]{0:T(1024)}, u32[]{:S(2)}) copy-start(f32[1024]{0:T(1024)} %param.13) | copy-start | bytes 12292
  530.4 9.6 %all-to-all-start.1 = ((bf16[2,64,1024]{2,1,0:T(8,128)(2,1)}), bf16[2,64,1024]{2,1,0:T(8,128)(2,1)}, u32[]{:S(2)}, u32[]{:S(2)}) async-start(bf16[2,64,1024]{2,1,0:T(8,128)(2,1)} %broadcast_select_fusion.2), calls=%async_computation.1 | async-start | bytes 524288 | tf_op jit(solution)/shard_map/all_to_all | solution.py:75
  560.4 9.6 %all-to-all-start.2 = ((bf16[2,64,1024]{2,1,0:T(8,128)(2,1)}), bf16[2,64,1024]{2,1,0:T(8,128)(2,1)}, u32[]{:S(2)}, u32[]{:S(2)}) async-start(bf16[2,64,1024]{2,1,0:T(8,128)(2,1)} %broadcast_select_fusion.1), calls=%async_computation.2 | async-start | bytes 524288 | tf_op jit(solution)/shard_map/all_to_all | solution.py:122
  564.5 86.4 %reduce-scatter.2.cloned.1.call-start = ((), (), s32[]{:S(2)}) async-start(), calls=%async_computation.5 | async-start | bytes 8192000 | tf_op jit(solution)/shard_map/reduce_scatter | solution.py:141
  589.5 0.6 copy-start.8
  589.5 0.7 copy-start.5
  589.6 61.4 %copy-start.2 = (f32[12800]{0:T(1024)S(1)}, f32[12800]{0:T(1024)}, u32[]{:S(2)}) copy-start(f32[12800]{0:T(1024)} %param.9) | copy-start | bytes 153604
Sparse Core Ops, SparseCore 0:
  9.6 502.7 all-gather.1
  589.7 61.2 reduce-scatter.1
where the time goes:
time: 664 us; the launch traced here: 663 us
  waiting for transfers between devices  552 us (83%)
  matrix products  29 us (4%)
  other arithmetic  26.1 us (4%)
  local copies, waits for them, and re-layouts  22.7 us (3%)
  between operations  14.2 us (2%)
  starting transfers between devices  12.7 us (2%)
    all_gather x1, waiting for transfers between devices, shards(): lax.all_gather(proj_weight, ('section', 'dp'), axis=0, tiled=True)  489 us
    reduce_scatter x1, waiting for transfers between devices, shards(): lax.psum_scatter(partial_grad, 'tensor', scatter_dimension=0, tiled=True)  57.1 us
    dot_general x1, matrix products, shards(): lax.dot_general(projected_grad, weight_all, contract_dims, preferred_elem...  15.9 us
  transfers between devices with their start and end apart: 5, of which 4 were waited for; matrix products, arithmetic and copies ran while one was open for 3% of the time, Pallas kernels for 0%

commit v1 on v0

--- a/solution.py
+++ b/solution.py
@@ -44,13 +44,27 @@
     lang_units = lang_total // UNIT
     capacity = unit_total // sections
     bucket_count = sections * capacity
-    vision_wide = vision_rows.astype(jnp.float32)
+    column_total = vision_rows.shape[1]
+    depth = proj_weight.shape[0]
+    parts = sections * groups
+    share = row_total // tensor_count
+    share_start = lax.axis_index("tensor") * share
+    own_rows = lax.dynamic_slice_in_dim(vision_rows, share_start, share, 0)
+    vision_wide = own_rows.astype(jnp.float32)
     centered = vision_wide - jnp.mean(vision_wide, axis=1, keepdims=True)
-    vision_inv = lax.rsqrt(jnp.mean(centered * centered, axis=1, keepdims=True) + VISION_EPS)
-    vision_hat = centered * vision_inv
-    normed_vision = (vision_hat * vision_gain + vision_bias).astype(jnp.bfloat16)
-    weight_all = lax.all_gather(proj_weight, ("section", "dp"), axis=0, tiled=True)
-    projected = jnp.dot(normed_vision, weight_all, preferred_element_type=jnp.float32)
+    own_inv = lax.rsqrt(jnp.mean(centered * centered, axis=1, keepdims=True) + VISION_EPS)
+    own_hat = centered * own_inv
+    normed_vision = (own_hat * vision_gain + vision_bias).astype(jnp.bfloat16)
+    outgoing = normed_vision.reshape(share, parts, depth).transpose(1, 0, 2)
+    incoming = lax.all_to_all(
+        outgoing, ("section", "dp"), split_axis=0, concat_axis=0, tiled=True
+    )
+    rows_all = lax.all_gather(incoming, "tensor", axis=1, tiled=True)
+    rows_all = rows_all.reshape(parts * row_total, depth)
+    partial_out = jnp.dot(rows_all, proj_weight, preferred_element_type=jnp.float32)
+    projected = lax.psum_scatter(
+        partial_out.astype(jnp.bfloat16), ("section", "dp"), scatter_dimension=0, tiled=True
+    ).astype(jnp.float32)
     features = gelu_value(projected).astype(jnp.bfloat16)
     unit_slot = slot_of_row.reshape(unit_total, UNIT)[:, 0]
     unit_live = unit_slot >= 0
@@ -106,11 +120,13 @@
         text_rows.reshape(lang_units, UNIT * column_count),
     )
     hidden_wide = hidden_units.reshape(lang_total, column_count).astype(jnp.float32)
-    square_total = lax.psum(jnp.sum(hidden_wide * hidden_wide, axis=1), "tensor")
+    upstream = out_cotangent.astype(jnp.float32) * text_gain
+    sums = jnp.stack(
+        [jnp.sum(hidden_wide * hidden_wide, axis=1), jnp.sum(upstream * hidden_wide, axis=1)]
+    )
+    square_total, cross_total = lax.psum(sums, "tensor")
     hidden_inv = lax.rsqrt(square_total / D + EPSILON)[:, None]
     normed = (hidden_wide * hidden_inv * text_gain).astype(jnp.bfloat16)
-    upstream = out_cotangent.astype(jnp.float32) * text_gain
-    cross_total = lax.psum(jnp.sum(upstream * hidden_wide, axis=1), "tensor")
     cross_mean = (cross_total / D)[:, None]
     hidden_grad = (
         hidden_inv * (upstream - hidden_wide * hidden_inv * hidden_inv * cross_mean)
@@ -132,15 +148,17 @@
     )
     feature_grad = feature_grad.reshape(row_total, column_count)
     projected_grad = (feature_grad.astype(jnp.float32) * gelu_slope(projected)).astype(jnp.bfloat16)
-    share = row_total // tensor_count
-    share_start = lax.axis_index("tensor") * share
+    grad_all = lax.all_gather(projected_grad, ("section", "dp"), axis=0, tiled=True)
     contract_dims = (((1,), (1,)), ((), ()))
     partial_grad = lax.dot_general(
-        projected_grad, weight_all, contract_dims, preferred_element_type=jnp.float32
+        grad_all, proj_weight, contract_dims, preferred_element_type=jnp.float32
     )
-    normed_grad = lax.psum_scatter(partial_grad, "tensor", scatter_dimension=0, tiled=True)
-    own_hat = lax.dynamic_slice_in_dim(vision_hat, share_start, share, 0)
-    own_inv = lax.dynamic_slice_in_dim(vision_inv, share_start, share, 0)
+    partial_grad = partial_grad.astype(jnp.bfloat16).reshape(parts, row_total, depth)
+    summed = lax.psum_scatter(partial_grad, "tensor", scatter_dimension=1, tiled=True)
+    gathered = lax.all_to_all(
+        summed, ("section", "dp"), split_axis=0, concat_axis=0, tiled=True
+    )
+    normed_grad = gathered.transpose(1, 0, 2).reshape(share, column_total).astype(jnp.float32)
     weighted = normed_grad * vision_gain
     weighted_mean = jnp.mean(weighted, axis=1, keepdims=True)
     vision_cross = jnp.mean(weighted * own_hat, axis=1, keepdims=True)

time: 664 us -> 361 us (0.54)
  waiting for transfers between devices: 552 us -> 200 us
  blocking collectives: 6.31 us -> 35.8 us
  local copies, waits for them, and re-layouts: 22.7 us -> 48.5 us
  matrix products: 29 us -> 12.6 us
    all_gather x1 -> x2, waiting for transfers between devices: 489 us -> 76 us  [the longest x1 47.9 us: shards(): lax.all_gather(projected_grad, ('section', 'dp'), axis=0, tiled=True)]
    reduce_scatter x1 -> x2, waiting for transfers between devices: 57.1 us -> 93.4 us  [the longest x1 55.1 us: shards(): lax.psum_scatter(partial_out.astype(jnp.bfloat16), ('section', 'dp'), sca...]
    all_to_all x0 -> x1, blocking collectives: none -> 29.5 us  [shards(): lax.all_to_all(outgoing, ('section', 'dp'), split_axis=0, concat_axis=0,...]
    all_to_all x0 -> x1, waiting for transfers between devices: none -> 22.4 us  [shards(): lax.all_to_all(summed, ('section', 'dp'), split_axis=0, concat_axis=0, ti...]
    dot_general x2, matrix products: 29 us -> 12.6 us  [the longest x1 7.22 us: shards(): jnp.dot(rows_all, proj_weight, preferred_element_type=jnp.float32)]
    reshape x0 -> x2, local copies, waits for them, and re-layouts: none -> 8.83 us  [the longest x1 6.24 us: shards(): partial_grad.astype(jnp.bfloat16).reshape(parts, row_total, depth)]
    convert_element_type x0 -> x4, other arithmetic: none -> 7.37 us  [the longest x1 2.4 us: shards(): normed_vision = (own_hat * vision_gain + vision_bias).astype(jnp.bfloat16)]
  transfers between devices with their start and end apart: 5 -> 8, of which waited for: 4 -> 8; matrix products, arithmetic and copies ran while one was open for 3% -> 3% of each run, Pallas kernels for 0% -> 0%
where the time goes in v1:
time: 361 us; the launch traced here: 360 us
  waiting for transfers between devices  200 us (55%)
  local copies, waits for them, and re-layouts  48.5 us (13%)
  blocking collectives  35.8 us (10%)
  other arithmetic  31.5 us (9%)
  starting transfers between devices  17.2 us (5%)
  between operations  14 us (4%)
  matrix products  12.6 us (3%)
    reduce_scatter x1, waiting for transfers between devices, shards(): lax.psum_scatter(partial_out.astype(jnp.bfloat16), ('section', 'dp'), sca...  55.1 us
    all_gather x1, waiting for transfers between devices, shards(): lax.all_gather(projected_grad, ('section', 'dp'), axis=0, tiled=True)  47.9 us
    reduce_scatter x1, waiting for transfers between devices, shards(): lax.psum_scatter(partial_grad, 'tensor', scatter_dimension=1, tiled=True)  38.3 us
    all_to_all x1, blocking collectives, shards(): lax.all_to_all(outgoing, ('section', 'dp'), split_axis=0, concat_axis=0,...  29.5 us
    all_gather x1, waiting for transfers between devices, shards(): rows_all = lax.all_gather(incoming, 'tensor', axis=1, tiled=True)  28.1 us
    all_to_all x1, waiting for transfers between devices, shards(): lax.all_to_all(summed, ('section', 'dp'), split_axis=0, concat_axis=0, ti...  22.4 us
    dot_general x1, matrix products, shards(): jnp.dot(rows_all, proj_weight, preferred_element_type=jnp.float32)  7.22 us
  transfers between devices with their start and end apart: 8, of which 8 were waited for; matrix products, arithmetic and copies ran while one was open for 3% of the time, Pallas kernels for 0%

profile of v1, /device:TPU:0, one launch (start us, length us, event | category | flops | bytes accessed | tf_op | source)
XLA Modules:
  0.0 359.6 jit_solution(12818028492465236369)
XLA Ops:
  7.3 1.5 convert_reduce_fusion
  8.8 1.5 fusion.19
  10.3 2.4 fusion.14
  12.7 2.6 reshape.339
  15.3 1.2 copy.71
  16.6 29.5 %all_to_all.26 = bf16[8,32,1600]{2,1,0:T(8,128)(2,1)S(1)} all-to-all(bf16[8,32,1600]{2,1,0:T(8,128)(2,1)S(1)} %copy.71), channel_id=1, replica_groups=mesh['section'=2,'dp'=4,'tensor'=4] {'section','dp'}, dimensions={0} | all-to-all | bytes 1638400 | tf_op jit(solution)/shard_map/all_to_all | solution.py:59
  46.0 1.2 copy.72
  47.3 28.1 %all-gather.3.cloned.1.call-done = bf16[8,128,1600]{2,0,1:T(8,128)(2,1)} async-done(((bf16[8,32,1600]{2,0,1:T(8,128)(2,1)}), bf16[8,128,1600]{2,0,1:T(8,128)(2,1)}) %all-gather.3.cloned.1.call-update) | async-done | bytes 3276816 | tf_op jit(solution)/shard_map/all_gather | solution.py:62
  75.4 6.2 %copy.73 = bf16[8,128,1600]{1,0,2:T(8,128)(2,1)} copy(bf16[8,128,1600]{2,0,1:T(8,128)(2,1)} %all-gather.3.cloned.1.call-done) | data formatting | bytes 6553600 | tf_op jit(solution)/shard_map/all_gather | solution.py:62
  81.6 7.2 %fusion.9 = bf16[1024,1024]{1,0:T(8,128)(2,1)} fusion(bf16[1600,1024]{1,0:T(8,128)(2,1)S(1)} %copy-done, bf16[200,8,8,128]{3,2,1,0:T(8,128)(2,1)} %bitcast.35), kind=kOutput, calls=%fused_computation.18 | convolution fusion | flops 3356491776 | bytes 8650752 | tf_op jit(solution)/shard_map/dot_general | solution.py:64
  90.9 3.2 all-to-all-start
  95.2 2.6 all-to-all-done
  101.9 55.1 %reduce-scatter.3.cloned.1.call-done = bf16[128,1024]{1,0:T(8,128)(2,1)} async-done(((bf16[1024,1024]{1,0:T(8,128)(2,1)}), bf16[128,1024]{1,0:T(8,128)(2,1)}) %reduce-scatter.3.cloned.1.call-update) | async-done | bytes 262160 | tf_op jit(solution)/shard_map/reduce_scatter | solution.py:65
  157.0 1.8 fusion.30
  158.8 1.1 reshape.341
  159.9 1.4 gather_fusion
  162.3 1.4 broadcast_select_fusion.2
  163.8 4.1 %all-to-all-start.2 = ((bf16[2,64,1024]{2,1,0:T(8,128)(2,1)}), bf16[2,64,1024]{2,1,0:T(8,128)(2,1)}, u32[]{:S(2)}, u32[]{:S(2)}) async-start(bf16[2,64,1024]{2,1,0:T(8,128)(2,1)} %broadcast_select_fusion.2), calls=%async_computation.3 | async-start | bytes 524288 | tf_op jit(solution)/shard_map/all_to_all | solution.py:89
  167.9 1.2 pad_clamp_fusion.2
  171.7 1.3 pad_clamp_fusion.1
  173.2 1.1 reshape.342
  174.2 1.5 gather_fusion.1
  175.8 1.8 gather.23
  177.6 2.0 fusion.27
  180.2 6.3 %psum.7 = f32[2,128]{1,0:T(2,128)} all-reduce(f32[2,128]{1,0:T(2,128)} %pad_maximum_fusion), channel_id=1, replica_groups=mesh['section'=2,'dp'=4,'tensor'=4] {'tensor'}, use_global_device_ids=true, to_apply=%region_11.12 | all-reduce | flops 256 | bytes 2048 | tf_op jit(solution)/shard_map/psum | solution.py:127
  187.3 2.0 fusion.26
  189.2 1.1 reshape.343
  190.3 1.5 gather_fusion.2
  192.9 1.4 broadcast_select_fusion.1
  194.3 4.1 %all-to-all-start.3 = ((bf16[2,64,1024]{2,1,0:T(8,128)(2,1)}), bf16[2,64,1024]{2,1,0:T(8,128)(2,1)}, u32[]{:S(2)}, u32[]{:S(2)}) async-start(bf16[2,64,1024]{2,1,0:T(8,128)(2,1)} %broadcast_select_fusion.1), calls=%async_computation.4 | async-start | bytes 524288 | tf_op jit(solution)/shard_map/all_to_all | solution.py:138
  198.8 5.4 %all-to-all-done.3 = bf16[2,64,1024]{2,1,0:T(8,128)(2,1)} async-done(((bf16[2,64,1024]{2,1,0:T(8,128)(2,1)}), bf16[2,64,1024]{2,1,0:T(8,128)(2,1)}, u32[]{:S(2)}, u32[]{:S(2)}) %all-to-all-start.3) | async-done | bytes 262176 | tf_op jit(solution)/shard_map/all_to_all | solution.py:138
  204.1 1.1 reshape.344
  205.2 1.4 gather_fusion.3
  207.7 1.9 fusion.37
  209.9 47.9 %all-gather.5.cloned.1.call-done = bf16[1024,1024]{1,0:T(8,128)(2,1)} async-done(((bf16[128,1024]{1,0:T(8,128)(2,1)}), bf16[1024,1024]{1,0:T(8,128)(2,1)}) %all-gather.5.cloned.1.call-update) | async-done | bytes 2097168 | tf_op jit(solution)/shard_map/all_gather | solution.py:151
  257.8 5.4 %fusion.8 = bf16[200,8,8,128]{3,1,2,0:T(8,128)(2,1)S(1)} fusion(bf16[1024,1024]{1,0:T(8,128)(2,1)} %all-gather.5.cloned.1.call-done, bf16[1600,1024]{1,0:T(8,128)(2,1)S(1)} %copy-done), kind=kOutput, calls=%fused_computation.17 | convolution fusion | flops 3357081600 | bytes 8650752 | tf_op jit(solution)/shard_map/dot_general | solution.py:153
  263.2 2.6 copy.90
  265.7 6.2 %copy.85 = bf16[8,128,1600]{2,0,1:T(8,128)(2,1)} copy(bf16[8,128,1600]{1,0,2:T(8,128)(2,1)} %bitcast.33) | data formatting | bytes 6553600 | tf_op jit(solution)/shard_map/reshape | solution.py:156
  272.0 38.3 %reduce-scatter.5.cloned.1.call-done = bf16[8,32,1600]{2,0,1:T(8,128)(2,1)} async-done(((bf16[8,128,1600]{2,0,1:T(8,128)(2,1)}), bf16[8,32,1600]{2,0,1:T(8,128)(2,1)}) %reduce-scatter.5.cloned.1.call-update) | async-done | bytes 819216 | tf_op jit(solution)/shard_map/reduce_scatter | solution.py:157
  310.3 2.1 copy.86
  312.4 5.5 %all-to-all-start.4 = ((bf16[8,32,1600]{2,1,0:T(8,128)(2,1)}), bf16[8,32,1600]{2,1,0:T(8,128)(2,1)}, u32[]{:S(2)}, u32[]{:S(2)}) async-start(bf16[8,32,1600]{2,1,0:T(8,128)(2,1)} %copy.86), calls=%async_computation.6 | async-start | bytes 1703936 | tf_op jit(solution)/shard_map/all_to_all | solution.py:158
  318.0 22.4 %all-to-all-done.4 = bf16[8,32,1600]{2,1,0:T(8,128)(2,1)} async-done(((bf16[8,32,1600]{2,1,0:T(8,128)(2,1)}), bf16[8,32,1600]{2,1,0:T(8,128)(2,1)}, u32[]{:S(2)}, u32[]{:S(2)}) %all-to-all-start.4) | async-done | bytes 819232 | tf_op jit(solution)/shard_map/all_to_all | solution.py:158
  340.5 1.3 convert_bitcast_fusion
  341.7 2.2 copy.87
  343.9 2.8 reshape.346
  346.8 2.2 fusion.15
  349.0 1.4 fusion.12
  350.5 2.6 fusion.18
  (81 shorter events, 15.4 us)
Async XLA Ops:
  7.2 74.5 %copy-start = (bf16[1600,1024]{1,0:T(8,128)(2,1)S(1)}, bf16[1600,1024]{1,0:T(8,128)(2,1)}, u32[]{:S(2)}) copy-start(bf16[1600,1024]{1,0:T(8,128)(2,1)} %param.11) | copy-start | bytes 9830404
  7.2 3.1 copy-start.5
  7.2 3.1 copy-start.3
  7.2 68.2 %all-gather.3.cloned.1.call-start = ((), (), s32[]{:S(2)}) async-start(), calls=%async_computation.7 | async-start | bytes 4259840 | tf_op jit(solution)/shard_map/all_gather | solution.py:62
  10.3 5.0 %copy-start.7 = (f32[32]{0:T(128)}, f32[32]{0:T(128)S(1)}, u32[]{:S(2)}) copy-start(f32[32]{0:T(128)S(1)} %add_rsqrt_fusion) | copy-start | bytes 388
  47.3 109.8 %reduce-scatter.3.cloned.1.call-start = ((), (), s32[]{:S(2)}) async-start(), calls=%async_computation.8 | async-start | bytes 2359296 | tf_op jit(solution)/shard_map/reduce_scatter | solution.py:65
  88.9 0.7 copy-start.11
  89.7 67.3 %copy-start.9 = (pred[8]{0:T(512)(128)(4,1)}, pred[8]{0:T(512)(128)(4,1)S(1)}, u32[]{:S(2)}) copy-start(pred[8]{0:T(512)(128)(4,1)S(1)} %get-tuple-element.12) | copy-start | bytes 28
  90.9 6.9 %all-to-all-start = ((s32[2,1,4]{2,1,0:T(1,128)}), s32[2,1,4]{2,1,0:T(1,128)S(1)}, u32[]{:S(2)}, u32[]{:S(2)}) async-start(s32[2,1,4]{2,1,0:T(1,128)} %bitcast), calls=%async_computation | async-start | bytes 2048 | tf_op jit(solution)/shard_map/all_to_all | solution.py:96
  163.8 9.4 %all-to-all-start.2 = ((bf16[2,64,1024]{2,1,0:T(8,128)(2,1)}), bf16[2,64,1024]{2,1,0:T(8,128)(2,1)}, u32[]{:S(2)}, u32[]{:S(2)}) async-start(bf16[2,64,1024]{2,1,0:T(8,128)(2,1)} %broadcast_select_fusion.2), calls=%async_computation.3 | async-start | bytes 524288 | tf_op jit(solution)/shard_map/all_to_all | solution.py:89
  173.0 4.6 %copy-start.6 = (f32[1024]{0:T(1024)S(1)}, f32[1024]{0:T(1024)}, u32[]{:S(2)}) copy-start(f32[1024]{0:T(1024)} %param.13) | copy-start | bytes 12292
  175.8 11.5 %copy-start.2 = (bf16[128,1024]{1,0:T(8,128)(2,1)S(1)}, bf16[128,1024]{1,0:T(8,128)(2,1)}, u32[]{:S(2)}) copy-start(bf16[128,1024]{1,0:T(8,128)(2,1)} %param.15) | copy-start | bytes 786436
  190.3 8.3 %copy-start.10 = (pred[8]{0:T(512)(128)(4,1)S(1)}, pred[8]{0:T(512)(128)(4,1)}, u32[]{:S(2)}) copy-start(pred[8]{0:T(512)(128)(4,1)} %copy-done.9) | copy-start | bytes 28
  194.3 9.8 %all-to-all-start.3 = ((bf16[2,64,1024]{2,1,0:T(8,128)(2,1)}), bf16[2,64,1024]{2,1,0:T(8,128)(2,1)}, u32[]{:S(2)}, u32[]{:S(2)}) async-start(bf16[2,64,1024]{2,1,0:T(8,128)(2,1)} %broadcast_select_fusion.1), calls=%async_computation.4 | async-start | bytes 524288 | tf_op jit(solution)/shard_map/all_to_all | solution.py:138
  198.4 59.3 %all-gather.5.cloned.1.call-start = ((), (), s32[]{:S(2)}) async-start(), calls=%async_computation.9 | async-start | bytes 2359296 | tf_op jit(solution)/shard_map/all_gather | solution.py:151
  209.7 100.6 %reduce-scatter.5.cloned.1.call-start = ((), (), s32[]{:S(2)}) async-start(), calls=%async_computation.10 | async-start | bytes 4259840 | tf_op jit(solution)/shard_map/reduce_scatter | solution.py:157
  272.0 45.9 %copy-start.4 = (f32[12800]{0:T(1024)S(1)}, f32[12800]{0:T(1024)}, u32[]{:S(2)}) copy-start(f32[12800]{0:T(1024)} %param.9) | copy-start | bytes 153604
  312.4 28.0 %all-to-all-start.4 = ((bf16[8,32,1600]{2,1,0:T(8,128)(2,1)}), bf16[8,32,1600]{2,1,0:T(8,128)(2,1)}, u32[]{:S(2)}, u32[]{:S(2)}) async-start(bf16[8,32,1600]{2,1,0:T(8,128)(2,1)} %copy.86), calls=%async_computation.6 | async-start | bytes 1703936 | tf_op jit(solution)/shard_map/all_to_all | solution.py:158
  343.9 2.8 copy-start.8
  346.8 3.7 %copy-start.1 = (f32[32,12800]{1,0:T(8,128)S(1)}, f32[32,12800]{1,0:T(8,128)}, u32[]{:S(2)}) copy-start(f32[32,12800]{1,0:T(8,128)} %reshape.346) | copy-start | bytes 4915204
Sparse Core Ops, SparseCore 0:
  47.4 27.9 all-gather.2
  89.0 67.9 reduce-scatter.2
  209.8 47.9 all-gather.4
  272.1 38.1 reduce-scatter.4

commit v2 on v1

--- a/solution.py
+++ b/solution.py
@@ -1,6 +1,10 @@
+import functools
+
 import jax
 import jax.numpy as jnp
 from jax import lax
+from jax.experimental import pallas as pl
+from jax.experimental.pallas import tpu as pltpu
 from jax.sharding import PartitionSpec as P
 
 D = 4096
@@ -22,6 +26,471 @@
         0.5 * (1.0 + lax.erf(values * HALF_ROOT))
         + values * jnp.exp(-0.5 * values * values) * INV_ROOT_TWO_PI
     )
+
+
+MESH = pl.DeviceIdType.MESH
+BF16 = jnp.bfloat16
+F32 = jnp.float32
+
+
+def exchange_kernel(
+    sections,
+    groups,
+    tensor_count,
+    x_in,
+    weight,
+    text,
+    gain,
+    slots_row,
+    slots_col,
+    cotangent,
+    normed_out,
+    grad_out,
+    x_all,
+    own,
+    part_send,
+    part_recv,
+    group_send,
+    group_recv,
+    slope,
+    features,
+    slots_all,
+    stats,
+    grads,
+    pg_all,
+    grad_part,
+    keep,
+    core_send,
+    core_recv,
+    y_send,
+    y_recv,
+    last_send,
+    last_recv,
+    x_ssem,
+    x_rsem,
+    fwd_ssem,
+    part_ssem,
+    part_rsem,
+    group_ssem,
+    group_rsem,
+    feat_ssem,
+    feat_rsem,
+    slot_ssem,
+    slot_rsem,
+    stat_ssem,
+    stat_rsem,
+    grad_ssem,
+    grad_rsem,
+    pgz_ssem,
+    pgx_ssem,
+    pg_rsem,
+    core_ssem,
+    core_rsem,
+    y_ssem,
+    y_rsem,
+    last_ssem,
+    last_rsem,
+):
+    S, G, T = sections, groups, tensor_count
+    N, Y = S * G, T // 2
+    s = lax.axis_index("section")
+    d = lax.axis_index("dp")
+    t = lax.axis_index("tensor")
+    y, c = t // 2, t % 2
+    me = s * G + d
+    mate = y * 2 + 1 - c
+    share, depth = x_in.shape[1], x_in.shape[2]
+    rows, cols = share * T, weight.shape[1]
+    lang = text.shape[0]
+
+    def send(src, dst, ssem, rsem, device):
+        pltpu.make_async_remote_copy(
+            src_ref=src,
+            dst_ref=dst,
+            send_sem=ssem,
+            recv_sem=rsem,
+            device_id=device,
+            device_id_type=MESH,
+        ).start()
+
+    def arrived(ref, sem):
+        pltpu.make_async_copy(ref, ref, sem).wait()
+
+    def loop(count, body):
+        def step(i, carry):
+            body(i)
+            return carry
+
+        lax.fori_loop(0, count, step, 0)
+
+    barrier = pltpu.get_barrier_semaphore()
+
+    def greet(i):
+        @pl.when(i != me)
+        def _():
+            pl.semaphore_signal(barrier, inc=1, device_id=(i // G, i % G, t), device_id_type=MESH)
+
+    loop(N, greet)
+    for dt in range(1, T):
+        pl.semaphore_signal(barrier, inc=1, device_id=(s, d, (t + dt) % T), device_id_type=MESH)
+    pl.semaphore_wait(barrier, N - 1 + T - 1)
+
+    def send_x(j):
+        to_s, to_d = (s + j % S + 1) % S, (d + j // S + 1) % G
+        k = to_s * G + to_d
+
+        @pl.when(k != me)
+        def _():
+            send(x_in.at[k], x_all.at[t, me], x_ssem.at[k], x_rsem.at[t, me], (to_s, to_d, t))
+
+    loop(N, send_x)
+    x_all[t, me] = x_in[me]
+
+    def forward_x(j):
+        k = ((s - j % S - 1 + S) % S) * G + (d - j // S - 1 + G) % G
+
+        @pl.when(k != me)
+        def _():
+            arrived(x_all.at[t, k], x_rsem.at[t, k])
+
+        block = x_all.at[t, k]
+        for dy in range(1, Y):
+            peer = ((y + dy) % Y) * 2 + c
+            send(block, block, fwd_ssem.at[dy, k], x_rsem.at[t, k], (s, d, peer))
+        send(block, block, fwd_ssem.at[0, k], x_rsem.at[t, k], (s, d, mate))
+
+    loop(N, forward_x)
+
+    def combine_group(j):
+        at_d = (d - j - 1 + G) % G
+        total = own[at_d]
+        for js in range(1, S):
+            arrived(part_recv.at[js - 1, at_d], part_rsem.at[js - 1, at_d])
+            total = total + part_recv[js - 1, at_d].astype(F32)
+
+        own[at_d] = total
+
+        @pl.when(j < G - 1)
+        def _():
+            group_send[at_d] = total.astype(BF16)
+            slot = (d - at_d + G) % G - 1
+            send(
+                group_send.at[at_d],
+                group_recv.at[slot],
+                group_ssem.at[at_d],
+                group_rsem.at[slot],
+                (s, at_d, t),
+            )
+
+    def project_group(j):
+        at_d = (d - j - 1 + G) % G
+
+        def project_block(i):
+            at_s = (s - i - 1 + S) % S
+            k = at_s * G + at_d
+            for dy in range(1, Y):
+                other = ((y + dy) % Y) * 2 + c
+                block = x_all.at[other, k]
+                arrived(block, x_rsem.at[other, k])
+                send(block, block, fwd_ssem.at[Y - 1 + dy, k], x_rsem.at[other, k], (s, d, mate))
+            for at_y in range(Y):
+                other = at_y * 2 + 1 - c
+                arrived(x_all.at[other, k], x_rsem.at[other, k])
+            block = x_all[:, k].reshape(rows, depth)
+            partial_out = jnp.dot(block, weight[...], preferred_element_type=F32)
+
+            @pl.when(at_s == s)
+            def _():
+                own[at_d] = partial_out
+
+            @pl.when(at_s != s)
+            def _():
+                part_send[k] = partial_out.astype(BF16)
+                slot = (s - at_s + S) % S - 1
+                send(
+                    part_send.at[k],
+                    part_recv.at[slot, at_d],
+                    part_ssem.at[k],
+                    part_rsem.at[slot, at_d],
+                    (at_s, d, t),
+                )
+
+        loop(S, project_block)
+
+    def project_step(j):
+        @pl.when(j < G)
+        def _():
+            project_group(j)
+
+        @pl.when(j > 0)
+        def _():
+            combine_group(j - 1)
+
+    loop(G + 1, project_step)
+
+    projected = own[d]
+    for slot in range(G - 1):
+        arrived(group_recv.at[slot], group_rsem.at[slot])
+        projected = projected + group_recv[slot].astype(F32)
+    features[0] = gelu_value(projected).astype(BF16)
+    slots_all[0] = slots_row[...]
+    for js in range(1, S):
+        peer = ((s + js) % S, d, t)
+        send(features.at[0], features.at[S - js], feat_ssem.at[js], feat_rsem.at[S - js], peer)
+        send(slots_row, slots_all.at[S - js], slot_ssem.at[js], slot_rsem.at[S - js], peer)
+    slope[...] = gelu_slope(projected)
+    for js in range(1, S):
+        arrived(features.at[js], feat_rsem.at[js])
+        arrived(slots_all.at[js], slot_rsem.at[js])
+
+    slot_ids = me * lang + lax.broadcasted_iota(jnp.int32, (lang, rows), 0)
+    placed = jnp.zeros((lang, cols), F32)
+    taken = jnp.zeros((lang, 1), F32)
+    for js in range(S):
+        chosen = jnp.where(slots_all[js][0:1, :] == slot_ids, 1.0, 0.0)
+        taken = taken + jnp.sum(chosen, axis=1, keepdims=True)
+        placed = placed + jnp.dot(
+            chosen.astype(BF16), features[js], preferred_element_type=F32
+        )
+    hidden = jnp.where(taken > 0.5, placed, text[...].astype(F32))
+    upstream = cotangent[...].astype(F32) * gain[...]
+    squares = jnp.sum(hidden * hidden, axis=1, keepdims=True)
+    crosses = jnp.sum(upstream * hidden, axis=1, keepdims=True)
+    lanes = lax.broadcasted_iota(jnp.int32, (lang, 128), 1)
+    stats[0] = jnp.where(lanes < 64, squares, crosses)
+    for dt in range(1, T):
+        peer = (s, d, (t + dt) % T)
+        send(stats.at[0], stats.at[T - dt], stat_ssem.at[dt], stat_rsem.at[T - dt], peer)
+    total = stats[0]
+    for dt in range(1, T):
+        arrived(stats.at[dt], stat_rsem.at[dt])
+        total = total + stats[dt]
+    hidden_inv = lax.rsqrt(total[:, 0:1] / D + EPSILON)
+    cross_mean = total[:, 64:65] / D
+    grads[0] = (
+        hidden_inv * (upstream - hidden * hidden_inv * hidden_inv * cross_mean)
+    ).astype(BF16)
+    for js in range(1, S):
+        peer = ((s + js) % S, d, t)
+        send(grads.at[0], grads.at[S - js], grad_ssem.at[js], grad_rsem.at[S - js], peer)
+    normed_out[...] = (hidden * hidden_inv * gain[...]).astype(BF16)
+
+    feature_grad = jnp.zeros((rows, cols), F32)
+    lane_ids = lax.broadcasted_iota(jnp.int32, (rows, lang), 1)
+    for js in range(S):
+        if js > 0:
+            arrived(grads.at[js], grad_rsem.at[js])
+        first = (((s + js) % S) * G + d) * lang
+        chosen = jnp.where(slots_col[...] == first + lane_ids, 1.0, 0.0).astype(BF16)
+        feature_grad = feature_grad + jnp.dot(chosen, grads[js], preferred_element_type=F32)
+    pg_all[me] = (feature_grad * slope[...]).astype(BF16)
+
+    for jd in range(1, G):
+        send(
+            pg_all.at[me],
+            pg_all.at[me],
+            pgz_ssem.at[jd],
+            pg_rsem.at[me],
+            (s, (d + jd) % G, t),
+        )
+
+    def reduce_cores(k):
+        arrived(core_recv.at[k], core_rsem.at[k])
+        for at_y in range(Y):
+            keep[k, at_y] = keep[k, at_y] + core_recv[k, at_y].astype(F32)
+        for dy in range(1, Y):
+            to_y = (y + dy) % Y
+            y_send[k, dy - 1] = keep[k, to_y].astype(BF16)
+            send(
+                y_send.at[k, dy - 1],
+                y_recv.at[k, Y - dy - 1],
+                y_ssem.at[k, dy - 1],
+                y_rsem.at[k, Y - dy - 1],
+                (s, d, to_y * 2 + c),
+            )
+
+    def spread_step(j):
+        at_d = (d - j + G) % G
+        mine = s * G + at_d
+
+        @pl.when(j < G)
+        def _():
+            @pl.when(j > 0)
+            def _():
+                arrived(pg_all.at[mine], pg_rsem.at[mine])
+
+            for js in range(1, S):
+                send(
+                    pg_all.at[mine],
+                    pg_all.at[mine],
+                    pgx_ssem.at[js, at_d],
+                    pg_rsem.at[mine],
+                    ((s + js) % S, d, t),
+                )
+
+            def back_block(i):
+                k = ((s + i) % S) * G + at_d
+
+                @pl.when(i > 0)
+                def _():
+                    arrived(pg_all.at[k], pg_rsem.at[k])
+
+                grad_part[...] = lax.dot_general(
+                    pg_all[k], weight[...], (((1,), (1,)), ((), ())), preferred_element_type=F32
+                ).reshape(Y, 2, share, depth)
+                for at_y in range(Y):
+                    keep[k, at_y] = grad_part[at_y, c]
+                    core_send[k, at_y] = grad_part[at_y, 1 - c].astype(BF16)
+                send(
+                    core_send.at[k], core_recv.at[k], core_ssem.at[k], core_rsem.at[k], (s, d, mate)
+                )
+
+            loop(S, back_block)
+
+        @pl.when(j > 0)
+        def _():
+            before = (d - j + 1 + G) % G
+            loop(S, lambda i: reduce_cores(((s + i) % S) * G + before))
+
+    loop(G + 1, spread_step)
+
+    def finish(j):
+        to_s, to_d = (s + j % S) % S, (d - j // S + G) % G
+        k = to_s * G + to_d
+        total = keep[k, y]
+        for dy in range(1, Y):
+            arrived(y_recv.at[k, dy - 1], y_rsem.at[k, dy - 1])
+            total = total + y_recv[k, dy - 1].astype(F32)
+        last_send[k] = total.astype(BF16)
+
+        @pl.when(k != me)
+        def _():
+            send(
+                last_send.at[k], last_recv.at[me], last_ssem.at[k], last_rsem.at[me], (to_s, to_d, t)
+            )
+
+    loop(N, finish)
+
+    def collect(k):
+        @pl.when(k != me)
+        def _():
+            arrived(last_recv.at[k], last_rsem.at[k])
+            grad_out[k] = last_recv[k]
+            arrived(last_send.at[k], last_ssem.at[k])
+            arrived(x_in.at[k], x_ssem.at[k])
+
+        for i in range(2 * Y - 1):
+            arrived(x_all.at[t, k], fwd_ssem.at[i, k])
+        arrived(core_send.at[k], core_ssem.at[k])
+        for dy in range(1, Y):
+            arrived(y_send.at[k, dy - 1], y_ssem.at[k, dy - 1])
+
+        @pl.when(k // G != s)
+        def _():
+            arrived(part_send.at[k], part_ssem.at[k])
+
+    grad_out[me] = last_send[me]
+    loop(N, collect)
+
+    def drain(k):
+        @pl.when(k != d)
+        def _():
+            arrived(group_send.at[k], group_ssem.at[k])
+
+        for js in range(1, S):
+            arrived(pg_all.at[me], pgx_ssem.at[js, k])
+
+    loop(G, drain)
+    for jd in range(1, G):
+        arrived(pg_all.at[me], pgz_ssem.at[jd])
+    for js in range(1, S):
+        arrived(features.at[0], feat_ssem.at[js])
+        arrived(slots_row, slot_ssem.at[js])
+        arrived(grads.at[0], grad_ssem.at[js])
+    for dt in range(1, T):
+        arrived(stats.at[0], stat_ssem.at[dt])
+
+
+def exchange(S, G, T, x_in, weight, text, gain, slots, cotangent):
+    N, Y = S * G, T // 2
+    share, depth = x_in.shape[1:]
+    rows = share * T
+    lang, cols = text.shape
+    slots_row = jnp.broadcast_to(slots[None, :], (8, rows))
+    slots_col = jnp.broadcast_to(slots[:, None], (rows, lang))
+    sem = pltpu.SemaphoreType.DMA
+    vmem = pltpu.VMEM
+    whole = pl.BlockSpec(memory_space=pltpu.VMEM)
+    return pl.pallas_call(
+        functools.partial(exchange_kernel, S, G, T),
+        out_shape=(
+            jax.ShapeDtypeStruct((lang, cols), BF16),
+            jax.ShapeDtypeStruct((N, share, depth), BF16),
+        ),
+        in_specs=[whole] * 7,
+        out_specs=(whole, whole),
+        scratch_shapes=[
+            vmem((T, N, share, depth), BF16),
+            vmem((G, rows, cols), F32),
+            vmem((N, rows, cols), BF16),
+            vmem((S - 1, G, rows, cols), BF16),
+            vmem((G, rows, cols), BF16),
+            vmem((G - 1, rows, cols), BF16),
+            vmem((rows, cols), F32),
+            vmem((S, rows, cols), BF16),
+            vmem((S, 8, rows), jnp.int32),
+            vmem((T, lang, 128), F32),
+            vmem((S, lang, cols), BF16),
+            vmem((N, rows, cols), BF16),
+            vmem((Y, 2, share, depth), F32),
+            vmem((N, Y, share, depth), F32),
+            vmem((N, Y, share, depth), BF16),
+            vmem((N, Y, share, depth), BF16),
+            vmem((N, Y - 1, share, depth), BF16),
+            vmem((N, Y - 1, share, depth), BF16),
+            vmem((N, share, depth), BF16),
+            vmem((N, share, depth), BF16),
+            sem((N,)),
+            sem((T, N)),
+            sem((2 * Y - 1, N)),
+            sem((N,)),
+            sem((S - 1, G)),
+            sem((G,)),
+            sem((G - 1,)),
+            sem((S,)),
+            sem((S,)),
+            sem((S,)),
+            sem((S,)),
+            sem((T,)),
+            sem((T,)),
+            sem((S,)),
+            sem((S,)),
+            sem((G,)),
+            sem((S, G)),
+            sem((N,)),
+            sem((N,)),
+            sem((N,)),
+            sem((N, Y - 1)),
+            sem((N, Y - 1)),
+            sem((N,)),
+            sem((N,)),
+        ],
+        compiler_params=pltpu.CompilerParams(
+            collective_id=0, has_side_effects=True, vmem_limit_bytes=58 * 1024 * 1024
+        ),
+        cost_estimate=pl.CostEstimate(
+            flops=4 * N * rows * depth * cols, bytes_accessed=16 * 1024 * 1024, transcendentals=0
+        ),
+    )(x_in, weight, text, gain[None, :], slots_row, slots_col, cotangent)
+
+
+def vision_backward(gathered, vision_gain, own_hat, own_inv):
+    normed_grad = gathered.transpose(1, 0, 2).reshape(own_hat.shape).astype(jnp.float32)
+    weighted = normed_grad * vision_gain
+    weighted_mean = jnp.mean(weighted, axis=1, keepdims=True)
+    vision_cross = jnp.mean(weighted * own_hat, axis=1, keepdims=True)
+    vision_grad = own_inv * (weighted - weighted_mean - own_hat * vision_cross)
+    return vision_grad.astype(jnp.bfloat16)
 
 
 def shards(
@@ -56,6 +525,19 @@
     own_hat = centered * own_inv
     normed_vision = (own_hat * vision_gain + vision_bias).astype(jnp.bfloat16)
     outgoing = normed_vision.reshape(share, parts, depth).transpose(1, 0, 2)
+    if min(sections, groups) > 1 and parts <= 8 and tensor_count == 4 and lang_total % 128 == 0:
+        normed, gathered = exchange(
+            sections,
+            groups,
+            tensor_count,
+            outgoing,
+            proj_weight,
+            text_rows,
+            text_gain,
+            slot_of_row,
+            out_cotangent,
+        )
+        return normed, vision_backward(gathered, vision_gain, own_hat, own_inv)
     incoming = lax.all_to_all(
         outgoing, ("section", "dp"), split_axis=0, concat_axis=0, tiled=True
     )
@@ -158,12 +640,7 @@
     gathered = lax.all_to_all(
         summed, ("section", "dp"), split_axis=0, concat_axis=0, tiled=True
     )
-    normed_grad = gathered.transpose(1, 0, 2).reshape(share, column_total).astype(jnp.float32)
-    weighted = normed_grad * vision_gain
-    weighted_mean = jnp.mean(weighted, axis=1, keepdims=True)
-    vision_cross = jnp.mean(weighted * own_hat, axis=1, keepdims=True)
-    vision_grad = own_inv * (weighted - weighted_mean - own_hat * vision_cross)
-    return (normed, vision_grad.astype(jnp.bfloat16))
+    return normed, vision_backward(gathered, vision_gain, own_hat, own_inv)
 
 
 def solution(mesh):

time: 361 us -> 153 us (0.42)
  waiting for transfers between devices: 200 us -> 0 us
  Pallas kernels: 0 us -> 136 us
  local copies, waits for them, and re-layouts: 48.5 us -> 5.25 us
  blocking collectives: 35.8 us -> 0 us
  other arithmetic: 31.5 us -> 11.4 us
  starting transfers between devices: 17.2 us -> 0 us
  between operations: 14 us -> 0.73 us
  matrix products: 12.6 us -> 0 us
    pallas_call x0 -> x1, Pallas kernels: none -> 136 us  [exchange(): pl.pallas_call(functools.partial(exchange_kernel, S, G, T), out_shape=(ja...]
    reduce_scatter x2 -> x0, waiting for transfers between devices: 93.4 us -> none  [the longest x1 55.1 us: shards(): lax.psum_scatter(partial_out.astype(jnp.bfloat16), ('section', 'dp'), sca...]
    all_gather x2 -> x0, waiting for transfers between devices: 76 us -> none  [the longest x1 47.9 us: shards(): lax.all_gather(projected_grad, ('section', 'dp'), axis=0, tiled=True)]
    all_to_all x4 -> x0, waiting for transfers between devices: 30.6 us -> none  [the longest x1 22.4 us: shards(): lax.all_to_all(summed, ('section', 'dp'), split_axis=0, concat_axis=0, ti...]
    all_to_all x1 -> x0, blocking collectives: 29.5 us -> none  [shards(): lax.all_to_all(outgoing, ('section', 'dp'), split_axis=0, concat_axis=0,...]
    all_to_all x4 -> x0, starting transfers between devices: 16.9 us -> none  [the longest x1 5.49 us: shards(): lax.all_to_all(summed, ('section', 'dp'), split_axis=0, concat_axis=0, ti...]
    dot_general x2 -> x0, matrix products: 12.6 us -> none  [the longest x1 7.22 us: shards(): jnp.dot(rows_all, proj_weight, preferred_element_type=jnp.float32)]
    gather x8 -> x0, local copies, waits for them, and re-layouts: 10.9 us -> none  [the longest x2 3.36 us: shards(): arrived_units[slot_source]]
  transfers between devices with their start and end apart: 8 -> 0, of which waited for: 8 -> 0; matrix products, arithmetic and copies ran while one was open for 3% -> 0% of each run, Pallas kernels for 0% -> 0%
where the time goes in v2:
time: 153 us
  Pallas kernels  136 us (89%)
  other arithmetic  11.4 us (7%)
  local copies, waits for them, and re-layouts  5.25 us (3%)
    pallas_call x1, Pallas kernels, exchange(): pl.pallas_call(functools.partial(exchange_kernel, S, G, T), out_shape=(ja...  136 us

profile of v2, /device:TPU:0, one launch (start us, length us, event | category | flops | bytes accessed | tf_op | source)
XLA Modules:
  0.0 153.1 jit_solution(6986179523157657496)
XLA Ops:
  0.6 0.0 copy-start
  0.6 0.0 copy-start.3
  0.7 0.0 copy-start.2
  0.7 1.4 convert_reduce_fusion
  2.0 1.5 %fusion.12 = f32[32]{0:T(128)S(1)} fusion(f32[32]{0:T(128)S(1)} %broadcast_multiply_fusion.2, bf16[128,12800]{1,0:T(8,128)(2,1)} %param.8, s32[]{:T(128)S(6)} %select_n.3), kind=kLoop, calls=%fused_computation.16 | loop fusion | flops 1638368 | bytes 819460 | tf_op jit(solution)/shard_map/reduce_sum | solution.py:524
  3.6 0.0 copy-done.3
  3.6 0.6 broadcast_in_dim.7.slots_row
  4.2 0.0 copy-done
  4.2 0.1 mul.60
  4.3 0.7 broadcast_in_dim.8.slots_col
  5.0 0.0 copy-done.2
  5.0 1.5 fusion.7
  6.5 0.7 reshape.38
  7.2 1.0 copy.13
  8.2 135.8 %shard_map.95 = (bf16[128,1024]{1,0:T(8,128)(2,1)}, bf16[8,32,1600]{2,1,0:T(8,128)(2,1)}) custom-call(bf16[8,32,1600]{2,1,0:T(8,128)(2,1)} %bitcast.6, bf16[1600,1024]{1,0:T(8,128)(2,1)} %weight.1, bf16[128,1024]{1,0:T(8,128)(2,1)} %text.1, f32[1,1024]{1,0:T(1,128)} %bitcast.7, s32[8,128]{1,0:T(8,128)} %broadcast_in_dim.7.slots_row, ...), custom_call_target="tpu_custom_call" | custom-call | flops 6710886400 | bytes 16777216 | tf_op jit(solution)/shard_map/pallas_call | solution.py:424
  144.0 1.4 fusion.5
  145.4 1.3 convert_bitcast_fusion
  146.7 1.0 copy.11
  147.7 0.5 reshape.39
  148.1 1.6 %fusion.8 = f32[32]{0:T(128)S(1)} fusion(f32[32,12800]{1,0:T(8,128)S(1)} %reshape.39, f32[12800]{0:T(1024)S(1)} %copy-done, f32[32]{0:T(128)S(1)} %add_rsqrt_fusion, f32[32]{0:T(128)S(1)} %broadcast_multiply_fusion.2, bf16[128,12800]{1,0:T(8,128)(2,1)} %param.8, s32[]{:T(128)S(6)} %select_n.3), kind=kLoop, calls=%fused_computation.12 | loop fusion | flops 2457568 | bytes 2509188 | tf_op jit(solution)/shard_map/reduce_sum | solution.py:491
  149.8 0.0 copy-start.1
  149.8 2.6 %fusion.11 = bf16[32,12800]{1,0:T(8,128)(2,1)} fusion(f32[32,12800]{1,0:T(8,128)S(1)} %reshape.39, f32[32]{0:T(128)S(1)} %get-tuple-element.6, f32[32]{0:T(128)S(1)} %get-tuple-element.7, f32[12800]{0:T(1024)S(1)} %copy-done, f32[32]{0:T(128)S(1)} %add_rsqrt_fusion, f32[32]{0:T(128)S(1)} %broadcast_multiply_fusion.2, bf16[128,12800]{1,0:T(8,128)(2,1)} %param.8, ...), kind=kLoop, calls=%fused_computation.15 | loop fusion | flops 3686400 | bytes 3328516 | tf_op jit(solution)/shard_map/convert_element_type | solution.py:493
  152.4 0.0 copy-done.1
  152.4 0.7 copy.15
  (3 shorter events, 0.0 us)
Async XLA Ops:
  0.6 3.6 %copy-start = (f32[12800]{0:T(1024)S(1)}, f32[12800]{0:T(1024)}, u32[]{:S(2)}) copy-start(f32[12800]{0:T(1024)} %param.9) | copy-start | bytes 153604
  0.6 2.9 %copy-start.3 = (s32[128]{0:T(128)S(1)}, s32[128]{0:T(128)}, u32[]{:S(2)}) copy-start(s32[128]{0:T(128)} %param.14) | copy-start | bytes 1540
  0.7 4.3 %copy-start.2 = (f32[12800]{0:T(1024)S(1)}, f32[12800]{0:T(1024)}, u32[]{:S(2)}) copy-start(f32[12800]{0:T(1024)} %param.10) | copy-start | bytes 153604
  149.8 2.6 %copy-start.1 = (bf16[128,1024]{1,0:T(8,128)(2,1)S(1)}, bf16[128,1024]{1,0:T(8,128)(2,1)}, u32[]{:S(2)}) copy-start(bf16[128,1024]{1,0:T(8,128)(2,1)} %get-tuple-element.10) | copy-start | bytes 786436

commit v3 on v2

--- a/solution.py
+++ b/solution.py
@@ -37,15 +37,21 @@
     sections,
     groups,
     tensor_count,
-    x_in,
+    vision,
+    vision_gain,
+    vision_bias,
     weight,
     text,
     gain,
-    slots_row,
-    slots_col,
+    slots,
     cotangent,
     normed_out,
     grad_out,
+    raw,
+    x_in,
+    hat,
+    inverse,
+    slots_row,
     x_all,
     own,
     part_send,
@@ -90,6 +96,7 @@
     y_rsem,
     last_ssem,
     last_rsem,
+    raw_sem,
 ):
     S, G, T = sections, groups, tensor_count
     N, Y = S * G, T // 2
@@ -100,6 +107,7 @@
     me = s * G + d
     mate = y * 2 + 1 - c
     share, depth = x_in.shape[1], x_in.shape[2]
+    column_total = vision.shape[1]
     rows, cols = share * T, weight.shape[1]
     lang = text.shape[0]
 
@@ -130,9 +138,29 @@
         def _():
             pl.semaphore_signal(barrier, inc=1, device_id=(i // G, i % G, t), device_id_type=MESH)
 
+    fetch = pltpu.make_async_copy(vision.at[pl.ds(t * share, share)], raw, raw_sem)
+    fetch.start()
     loop(N, greet)
     for dt in range(1, T):
         pl.semaphore_signal(barrier, inc=1, device_id=(s, d, (t + dt) % T), device_id_type=MESH)
+    fetch.wait()
+    sums = jnp.zeros((share, 128), F32)
+    for at in range(0, column_total, 128):
+        sums = sums + raw[:, at : at + 128].astype(F32)
+    mean = jnp.sum(sums, axis=1, keepdims=True) / column_total
+    sums = jnp.zeros((share, 128), F32)
+    for at in range(0, column_total, 128):
+        centered = raw[:, at : at + 128].astype(F32) - mean
+        sums = sums + centered * centered
+    square_mean = jnp.sum(sums, axis=1, keepdims=True) / column_total
+    inverse[...] = jnp.broadcast_to(lax.rsqrt(square_mean + VISION_EPS), (share, 128))
+    own_inv = inverse[:, 0:1]
+    for n in range(N):
+        span = slice(n * depth, (n + 1) * depth)
+        own_hat = (raw[:, span].astype(F32) - mean) * own_inv
+        hat[n] = own_hat
+        x_in[n] = (own_hat * vision_gain[:, span] + vision_bias[:, span]).astype(BF16)
+    slots_row[...] = jnp.broadcast_to(slots[...], (8, rows))
     pl.semaphore_wait(barrier, N - 1 + T - 1)
 
     def send_x(j):
@@ -257,7 +285,7 @@
     squares = jnp.sum(hidden * hidden, axis=1, keepdims=True)
     crosses = jnp.sum(upstream * hidden, axis=1, keepdims=True)
     lanes = lax.broadcasted_iota(jnp.int32, (lang, 128), 1)
-    stats[0] = jnp.where(lanes < 64, squares, crosses)
+    stats[0] = jnp.where(lanes % 8 < 4, squares, crosses).T[0:8]
     for dt in range(1, T):
         peer = (s, d, (t + dt) % T)
         send(stats.at[0], stats.at[T - dt], stat_ssem.at[dt], stat_rsem.at[T - dt], peer)
@@ -265,8 +293,9 @@
     for dt in range(1, T):
         arrived(stats.at[dt], stat_rsem.at[dt])
         total = total + stats[dt]
+    total = jnp.concatenate([total] * (128 // 8), axis=0).T
     hidden_inv = lax.rsqrt(total[:, 0:1] / D + EPSILON)
-    cross_mean = total[:, 64:65] / D
+    cross_mean = total[:, 4:5] / D
     grads[0] = (
         hidden_inv * (upstream - hidden * hidden_inv * hidden_inv * cross_mean)
     ).astype(BF16)
@@ -277,11 +306,12 @@
 
     feature_grad = jnp.zeros((rows, cols), F32)
     lane_ids = lax.broadcasted_iota(jnp.int32, (rows, lang), 1)
+    slots_col = jnp.broadcast_to(slots[...], (rows, rows)).T
     for js in range(S):
         if js > 0:
             arrived(grads.at[js], grad_rsem.at[js])
         first = (((s + js) % S) * G + d) * lang
-        chosen = jnp.where(slots_col[...] == first + lane_ids, 1.0, 0.0).astype(BF16)
+        chosen = jnp.where(slots_col == first + lane_ids, 1.0, 0.0).astype(BF16)
         feature_grad = feature_grad + jnp.dot(chosen, grads[js], preferred_element_type=F32)
     pg_all[me] = (feature_grad * slope[...]).astype(BF16)
 
@@ -375,7 +405,6 @@
         @pl.when(k != me)
         def _():
             arrived(last_recv.at[k], last_rsem.at[k])
-            grad_out[k] = last_recv[k]
             arrived(last_send.at[k], last_ssem.at[k])
             arrived(x_in.at[k], x_ssem.at[k])
 
@@ -389,8 +418,22 @@
         def _():
             arrived(part_send.at[k], part_ssem.at[k])
 
-    grad_out[me] = last_send[me]
+    last_recv[me] = last_send[me]
     loop(N, collect)
+    plain = jnp.zeros((share, 1), F32)
+    crossed = jnp.zeros((share, 1), F32)
+    for n in range(N):
+        span = slice(n * depth, (n + 1) * depth)
+        weighted = last_recv[n].astype(F32) * vision_gain[:, span]
+        plain = plain + jnp.sum(weighted, axis=1, keepdims=True)
+        crossed = crossed + jnp.sum(weighted * hat[n], axis=1, keepdims=True)
+    plain = plain / column_total
+    crossed = crossed / column_total
+    own_inv = inverse[:, 0:1]
+    for n in range(N):
+        span = slice(n * depth, (n + 1) * depth)
+        weighted = last_recv[n].astype(F32) * vision_gain[:, span]
+        grad_out[:, span] = (own_inv * (weighted - plain - hat[n] * crossed)).astype(BF16)
 
     def drain(k):
         @pl.when(k != d)
@@ -411,13 +454,13 @@
         arrived(stats.at[0], stat_ssem.at[dt])
 
 
-def exchange(S, G, T, x_in, weight, text, gain, slots, cotangent):
+def exchange(
+    S, G, T, vision, vision_gain, vision_bias, weight, text, gain, slots, cotangent
+):
     N, Y = S * G, T // 2
-    share, depth = x_in.shape[1:]
-    rows = share * T
+    rows, column_total = vision.shape
+    share, depth = rows // T, weight.shape[0]
     lang, cols = text.shape
-    slots_row = jnp.broadcast_to(slots[None, :], (8, rows))
-    slots_col = jnp.broadcast_to(slots[:, None], (rows, lang))
     sem = pltpu.SemaphoreType.DMA
     vmem = pltpu.VMEM
     whole = pl.BlockSpec(memory_space=pltpu.VMEM)
@@ -425,11 +468,16 @@
         functools.partial(exchange_kernel, S, G, T),
         out_shape=(
             jax.ShapeDtypeStruct((lang, cols), BF16),
-            jax.ShapeDtypeStruct((N, share, depth), BF16),
+            jax.ShapeDtypeStruct((share, column_total), BF16),
         ),
-        in_specs=[whole] * 7,
+        in_specs=[pl.BlockSpec(memory_space=pl.ANY)] + [whole] * 7,
         out_specs=(whole, whole),
         scratch_shapes=[
+            vmem((share, column_total), BF16),
+            vmem((N, share, depth), BF16),
+            vmem((N, share, depth), F32),
+            vmem((share, 128), F32),
+            vmem((8, rows), jnp.int32),
             vmem((T, N, share, depth), BF16),
             vmem((G, rows, cols), F32),
             vmem((N, rows, cols), BF16),
@@ -439,7 +487,7 @@
             vmem((rows, cols), F32),
             vmem((S, rows, cols), BF16),
             vmem((S, 8, rows), jnp.int32),
-            vmem((T, lang, 128), F32),
+            vmem((T, 8, lang), F32),
             vmem((S, lang, cols), BF16),
             vmem((N, rows, cols), BF16),
             vmem((Y, 2, share, depth), F32),
@@ -474,6 +522,7 @@
             sem((N, Y - 1)),
             sem((N,)),
             sem((N,)),
+            sem,
         ],
         compiler_params=pltpu.CompilerParams(
             collective_id=0, has_side_effects=True, vmem_limit_bytes=58 * 1024 * 1024
@@ -481,7 +530,16 @@
         cost_estimate=pl.CostEstimate(
             flops=4 * N * rows * depth * cols, bytes_accessed=16 * 1024 * 1024, transcendentals=0
         ),
-    )(x_in, weight, text, gain[None, :], slots_row, slots_col, cotangent)
+    )(
+        vision,
+        vision_gain[None, :],
+        vision_bias[None, :],
+        weight,
+        text,
+        gain[None, :],
+        slots[None, :],
+        cotangent,
+    )
 
 
 def vision_backward(gathered, vision_gain, own_hat, own_inv):
@@ -516,6 +574,27 @@
     column_total = vision_rows.shape[1]
     depth = proj_weight.shape[0]
     parts = sections * groups
+    if (
+        min(sections, groups) > 1
+        and parts <= 8
+        and tensor_count == 4
+        and row_total == 128
+        and lang_total == 128
+        and column_total % 128 == 0
+    ):
+        return exchange(
+            sections,
+            groups,
+            tensor_count,
+            vision_rows,
+            vision_gain,
+            vision_bias,
+            proj_weight,
+            text_rows,
+            text_gain,
+            slot_of_row,
+            out_cotangent,
+        )
     share = row_total // tensor_count
     share_start = lax.axis_index("tensor") * share
     own_rows = lax.dynamic_slice_in_dim(vision_rows, share_start, share, 0)
@@ -525,19 +604,6 @@
     own_hat = centered * own_inv
     normed_vision = (own_hat * vision_gain + vision_bias).astype(jnp.bfloat16)
     outgoing = normed_vision.reshape(share, parts, depth).transpose(1, 0, 2)
-    if min(sections, groups) > 1 and parts <= 8 and tensor_count == 4 and lang_total % 128 == 0:
-        normed, gathered = exchange(
-            sections,
-            groups,
-            tensor_count,
-            outgoing,
-            proj_weight,
-            text_rows,
-            text_gain,
-            slot_of_row,
-            out_cotangent,
-        )
-        return normed, vision_backward(gathered, vision_gain, own_hat, own_inv)
     incoming = lax.all_to_all(
         outgoing, ("section", "dp"), split_axis=0, concat_axis=0, tiled=True
     )

time: 153 us -> 141 us (0.922)
  other arithmetic: 11.4 us -> 0 us
  Pallas kernels: 136 us -> 134 us
    reduce_sum x4 -> x0, other arithmetic: 5.96 us -> none  [the longest x1 1.62 us: vision_backward(): vision_cross = jnp.mean(weighted * own_hat, axis=1, keepdims=True)]
    convert_element_type x3 -> x0, other arithmetic: 5.37 us -> none  [the longest x1 2.59 us: vision_backward(): return vision_grad.astype(jnp.bfloat16)]
    unnamed x9 -> x2, local copies, waits for them, and re-layouts: 0.72 us -> 3.76 us
    pallas_call x1, Pallas kernels: 136 us -> 134 us  [exchange(): pl.pallas_call(functools.partial(exchange_kernel, S, G, T), out_shape=(ja...]
    reshape x2 -> x0, local copies, waits for them, and re-layouts: 1.68 us -> none  [shards(): outgoing = normed_vision.reshape(share, parts, depth).transpose(1, 0, 2)]
    broadcast_in_dim x2, local copies, waits for them, and re-layouts: 1.31 us -> 2.93 us  [the longest x1 1.47 us: exchange(): vision_gain[None, :]]
where the time goes in v3:
time: 141 us
  Pallas kernels  134 us (95%)
  local copies, waits for them, and re-layouts  6.69 us (5%)
    pallas_call x1, Pallas kernels, exchange(): pl.pallas_call(functools.partial(exchange_kernel, S, G, T), out_shape=(ja...  134 us
    unnamed x2, local copies, waits for them, and re-layouts  3.76 us

profile of v3, /device:TPU:0, one launch (start us, length us, event | category | flops | bytes accessed | tf_op | source)
XLA Modules:
  0.0 141.0 jit_solution(17682661704953316757)
XLA Ops:
  0.6 1.5 %broadcast_in_dim.12.vision_gain = f32[1,12800]{1,0:T(1,128)} reshape(f32[12800]{0:T(1024)} %param.9) | data formatting | bytes 102400 | tf_op jit(solution)/shard_map/broadcast_in_dim | solution.py:535
  2.1 1.5 %broadcast_in_dim.13.vision_bias = f32[1,12800]{1,0:T(1,128)} reshape(f32[12800]{0:T(1024)} %param.10) | data formatting | bytes 102400 | tf_op jit(solution)/shard_map/broadcast_in_dim | solution.py:536
  3.6 133.7 %shard_map.95 = (bf16[128,1024]{1,0:T(8,128)(2,1)}, bf16[32,12800]{1,0:T(8,128)(2,1)}) custom-call(bf16[128,12800]{1,0:T(8,128)(2,1)} %vision.1, f32[1,12800]{1,0:T(1,128)} %broadcast_in_dim.12.vision_gain, f32[1,12800]{1,0:T(1,128)} %broadcast_in_dim.13.vision_bias, bf16[1600,1024]{1,0:T(8,128)(2,1)} %weight.1, bf16[128,1024]{1,0:T(8,128)(2,1)} %text.1, ...), custom_call_target="tpu_custom_call" | custom-call | flops 6710886400 | bytes 16777216 | tf_op jit(solution)/shard_map/pallas_call | solution.py:467
  137.2 1.7 %copy.12 = bf16[128,1024]{1,0:T(8,128)(2,1)} copy(bf16[128,1024]{1,0:T(8,128)(2,1)} %get-tuple-element.4) | data formatting | bytes 524288
  138.9 2.1 %copy.13 = bf16[32,12800]{1,0:T(8,128)(2,1)} copy(bf16[32,12800]{1,0:T(8,128)(2,1)} %get-tuple-element.5) | data formatting | bytes 1638400

commit v4 on v1

--- a/solution.py
+++ b/solution.py
@@ -1,6 +1,10 @@
+import functools
+
 import jax
 import jax.numpy as jnp
 from jax import lax
+from jax.experimental import pallas as pl
+from jax.experimental.pallas import tpu as pltpu
 from jax.sharding import PartitionSpec as P
 
 D = 4096
@@ -22,6 +26,631 @@
         0.5 * (1.0 + lax.erf(values * HALF_ROOT))
         + values * jnp.exp(-0.5 * values * values) * INV_ROOT_TWO_PI
     )
+
+
+MESH = pl.DeviceIdType.MESH
+BF16 = jnp.bfloat16
+F32 = jnp.float32
+WAVES = 2
+
+
+def exchange_kernel(
+    sections,
+    groups,
+    tensor_count,
+    vision,
+    vision_gain,
+    vision_bias,
+    weight,
+    text,
+    gain,
+    slots,
+    cotangent,
+    normed_out,
+    grad_out,
+    raw,
+    x_in,
+    hat,
+    inverse,
+    slots_row,
+    x_all,
+    product,
+    own,
+    part_send,
+    part_recv,
+    group_send,
+    group_recv,
+    slope,
+    features,
+    slots_all,
+    hidden_all,
+    stats,
+    reply_send,
+    reply_recv,
+    pg_all,
+    grad_part,
+    keep,
+    core_send,
+    core_recv,
+    y_send,
+    y_recv,
+    last_send,
+    last_recv,
+    x_ssem,
+    x_rsem,
+    fwd_ssem,
+    part_ssem,
+    part_rsem,
+    group_ssem,
+    group_rsem,
+    feat_ssem,
+    feat_rsem,
+    slot_ssem,
+    slot_rsem,
+    stat_ssem,
+    stat_rsem,
+    reply_ssem,
+    reply_rsem,
+    pgz_ssem,
+    pgx_ssem,
+    pg_rsem,
+    core_ssem,
+    core_rsem,
+    y_ssem,
+    y_rsem,
+    last_ssem,
+    last_rsem,
+    raw_sem,
+):
+    S, G, T, W = sections, groups, tensor_count, WAVES
+    N, Y = S * G, T // 2
+    s = lax.axis_index("section")
+    d = lax.axis_index("dp")
+    t = lax.axis_index("tensor")
+    y, c = t // 2, t % 2
+    me = s * G + d
+    mate = y * 2 + 1 - c
+    depth, cols = weight.shape
+    column_total = vision.shape[1]
+    share = raw.shape[0]
+    piece = share // W
+    rows = piece * T
+    lang = text.shape[0]
+
+    def send(src, dst, ssem, rsem, device):
+        pltpu.make_async_remote_copy(
+            src_ref=src,
+            dst_ref=dst,
+            send_sem=ssem,
+            recv_sem=rsem,
+            device_id=device,
+            device_id_type=MESH,
+        ).start()
+
+    def arrived(ref, sem):
+        pltpu.make_async_copy(ref, ref, sem).wait()
+
+    def loop(first, last, body):
+        def step(i, carry):
+            body(i)
+            return carry
+
+        lax.fori_loop(first, last, step, 0)
+
+    def stage(q, body):
+        @pl.when((q >= 0) & (q < W * G))
+        def _():
+            body(q // G, q % G)
+
+    barrier = pltpu.get_barrier_semaphore()
+
+    def greet(i):
+        @pl.when(i != me)
+        def _():
+            pl.semaphore_signal(barrier, inc=1, device_id=(i // G, i % G, t), device_id_type=MESH)
+
+    fetch = pltpu.make_async_copy(vision.at[pl.ds(t * share, share)], raw, raw_sem)
+    fetch.start()
+    loop(0, N, greet)
+    for dt in range(1, T):
+        pl.semaphore_signal(barrier, inc=1, device_id=(s, d, (t + dt) % T), device_id_type=MESH)
+    fetch.wait()
+    sums = jnp.zeros((share, 128), F32)
+    for at in range(0, column_total, 128):
+        sums = sums + raw[:, at : at + 128].astype(F32)
+    mean = jnp.sum(sums, axis=1, keepdims=True) / column_total
+    sums = jnp.zeros((share, 128), F32)
+    for at in range(0, column_total, 128):
+        centered = raw[:, at : at + 128].astype(F32) - mean
+        sums = sums + centered * centered
+    square_mean = jnp.sum(sums, axis=1, keepdims=True) / column_total
+    inverse[...] = jnp.broadcast_to(lax.rsqrt(square_mean + VISION_EPS), (share, 128))
+    own_inv = inverse[:, 0:1]
+    for n in range(N):
+        span = slice(n * depth, (n + 1) * depth)
+        own_hat = (raw[:, span].astype(F32) - mean) * own_inv
+        hat[n] = own_hat
+        x_in[n] = (
+            (own_hat * vision_gain[:, span] + vision_bias[:, span])
+            .astype(BF16)
+            .reshape(W, piece, depth)
+        )
+    slots_row[...] = jnp.full(slots_row.shape, -1, jnp.int32)
+    slots_row[0:W] = slots[...]
+    slots_all[0] = slots_row[...]
+    pl.semaphore_wait(barrier, N - 1 + T - 1)
+
+    def send_x(i):
+        w, j = i // N, i % N
+        to_s, to_d = (s + j % S + 1) % S, (d + j // S + 1) % G
+        n = to_s * G + to_d
+        k = w * N + d * S + s
+
+        @pl.when(n != me)
+        def _():
+            send(
+                x_in.at[n, w],
+                x_all.at[k, t],
+                x_ssem.at[w * N + n],
+                x_rsem.at[k, t],
+                (to_s, to_d, t),
+            )
+
+    loop(0, W * N, send_x)
+    for w in range(W):
+        x_all[w * N + d * S + s, t] = x_in[me, w]
+    for js in range(1, S):
+        peer = ((s + js) % S, d, t)
+        send(slots_row, slots_all.at[S - js], slot_ssem.at[js], slot_rsem.at[S - js], peer)
+
+    def forward_group(w, j):
+        at_d = (d - j - 1 + G) % G
+
+        def forward_block(i):
+            at_s = (s - i - 1 + S) % S
+            k = (w * G + at_d) * S + at_s
+            block = x_all.at[k, t]
+
+            @pl.when((at_d != d) | (at_s != s))
+            def _():
+                arrived(block, x_rsem.at[k, t])
+
+            for dy in range(1, Y):
+                peer = ((y + dy) % Y) * 2 + c
+                send(block, block, fwd_ssem.at[dy, k], x_rsem.at[k, t], (s, d, peer))
+            send(block, block, fwd_ssem.at[0, k], x_rsem.at[k, t], (s, d, mate))
+
+        loop(0, S, forward_block)
+
+    def mate_group(w, j):
+        at_d = (d - j - 1 + G) % G
+
+        def mate_block(i):
+            k = (w * G + at_d) * S + i
+            for dy in range(1, Y):
+                other = ((y + dy) % Y) * 2 + c
+                block = x_all.at[k, other]
+                arrived(block, x_rsem.at[k, other])
+                send(block, block, fwd_ssem.at[Y - 1 + dy, k], x_rsem.at[k, other], (s, d, mate))
+
+        loop(0, S, mate_block)
+
+    def project_group(w, j):
+        at_d = (d - j - 1 + G) % G
+        at = w * G + at_d
+
+        def mate_arrived(i):
+            for at_y in range(Y):
+                other = at_y * 2 + 1 - c
+                arrived(x_all.at[at * S + i, other], x_rsem.at[at * S + i, other])
+
+        loop(0, S, mate_arrived)
+        block = x_all[pl.ds(at * S, S)].reshape(S * rows, depth)
+        product[...] = jnp.dot(block, weight[...], preferred_element_type=F32).reshape(
+            S, rows, cols
+        )
+        own[at] = product[s]
+        for js in range(1, S):
+            at_s = (s + js) % S
+            part_send[at, js - 1] = product[at_s].astype(BF16)
+            send(
+                part_send.at[at, js - 1],
+                part_recv.at[S - js - 1, at],
+                part_ssem.at[js - 1, at],
+                part_rsem.at[S - js - 1, at],
+                (at_s, d, t),
+            )
+
+    def combine_group(w, j):
+        at_d = (d - j - 1 + G) % G
+        at = w * G + at_d
+        total = own[at]
+        for js in range(1, S):
+            arrived(part_recv.at[js - 1, at], part_rsem.at[js - 1, at])
+            total = total + part_recv[js - 1, at].astype(F32)
+
+        own[at] = total
+
+        @pl.when(at_d != d)
+        def _():
+            group_send[at] = total.astype(BF16)
+            slot = (d - at_d + G) % G - 1
+            send(
+                group_send.at[at],
+                group_recv.at[w, slot],
+                group_ssem.at[at],
+                group_rsem.at[w, slot],
+                (s, at_d, t),
+            )
+
+    def forward_tick(q):
+        stage(q, forward_group)
+        stage(q - 1, mate_group)
+        stage(q - 2, project_group)
+        stage(q - 3, combine_group)
+
+    def finish_projection(w):
+        projected = own[w * G + d]
+        for slot in range(G - 1):
+            arrived(group_recv.at[w, slot], group_rsem.at[w, slot])
+            projected = projected + group_recv[w, slot].astype(F32)
+        features[w, 0] = gelu_value(projected).astype(BF16)
+        for js in range(1, S):
+            peer = ((s + js) % S, d, t)
+            send(
+                features.at[w, 0],
+                features.at[w, S - js],
+                feat_ssem.at[w, js],
+                feat_rsem.at[w, S - js],
+                peer,
+            )
+        slope[w] = gelu_slope(projected)
+
+    def placement(w):
+        slot_ids = me * lang + lax.broadcasted_iota(jnp.int32, (lang, rows), 0)
+        placed = jnp.zeros((lang, cols), F32)
+        taken = jnp.zeros((lang, 1), F32)
+        for js in range(S):
+            if js > 0:
+                arrived(features.at[w, js], feat_rsem.at[w, js])
+            chosen = jnp.where(slots_all[js, w : w + 1, :] == slot_ids, 1.0, 0.0)
+            taken = taken + jnp.sum(chosen, axis=1, keepdims=True)
+            placed = placed + jnp.dot(
+                chosen.astype(BF16), features[w, js], preferred_element_type=F32
+            )
+        hidden = jnp.where(taken > 0.5, placed, text[...].astype(F32))
+        hidden_all[w] = hidden
+        upstream = cotangent[...].astype(F32) * gain[...]
+        squares = jnp.sum(hidden * hidden, axis=1, keepdims=True)
+        crosses = jnp.sum(upstream * hidden, axis=1, keepdims=True)
+        lanes = lax.broadcasted_iota(jnp.int32, (lang, 128), 1)
+        stats[w, 0] = jnp.where(lanes % 8 < 4, squares, crosses).T[0:8]
+        for dt in range(1, T):
+            send(
+                stats.at[w, 0],
+                stats.at[w, T - dt],
+                stat_ssem.at[w, dt],
+                stat_rsem.at[w, T - dt],
+                (s, d, (t + dt) % T),
+            )
+        return taken
+
+    def reply(w, taken):
+        total = stats[w, 0]
+        for dt in range(1, T):
+            arrived(stats.at[w, dt], stat_rsem.at[w, dt])
+            total = total + stats[w, dt]
+        total = jnp.concatenate([total] * (128 // 8), axis=0).T
+        hidden_inv = lax.rsqrt(total[:, 0:1] / D + EPSILON)
+        cross_mean = total[:, 4:5] / D
+        hidden = hidden_all[w]
+        upstream = cotangent[...].astype(F32) * gain[...]
+        grads = (
+            hidden_inv * (upstream - hidden * hidden_inv * hidden_inv * cross_mean)
+        ).astype(BF16)
+        lane_ids = me * lang + lax.broadcasted_iota(jnp.int32, (rows, lang), 1)
+        for js in reversed(range(S)):
+            named = slots_all[js, w : w + 1, :]
+            named = jnp.concatenate([named] * (128 // rows), axis=1)
+            named = jnp.broadcast_to(named, (128, 128)).T[0:rows]
+            chosen = jnp.where(named == lane_ids, 1.0, 0.0).astype(BF16)
+            answer = jnp.dot(chosen, grads, preferred_element_type=F32).astype(BF16)
+            if js == 0:
+                reply_recv[w, 0] = answer
+            else:
+                reply_send[w, js] = answer
+                send(
+                    reply_send.at[w, js],
+                    reply_recv.at[w, S - js],
+                    reply_ssem.at[w, js],
+                    reply_rsem.at[w, S - js],
+                    ((s + js) % S, d, t),
+                )
+        normed = (hidden * hidden_inv * gain[...]).astype(BF16)
+        if w > 0:
+            normed = jnp.where(taken > 0.5, normed.astype(F32), normed_out[...].astype(F32))
+        normed_out[...] = normed.astype(BF16)
+
+    def start_back(w):
+        feature_grad = reply_recv[w, 0].astype(F32)
+        for js in range(1, S):
+            arrived(reply_recv.at[w, js], reply_rsem.at[w, js])
+            feature_grad = feature_grad + reply_recv[w, js].astype(F32)
+        k = (w * G + d) * S + s
+        pg_all[k] = (feature_grad * slope[w]).astype(BF16)
+        for jd in range(1, G):
+            send(
+                pg_all.at[k],
+                pg_all.at[k],
+                pgz_ssem.at[w, jd],
+                pg_rsem.at[k],
+                (s, (d + jd) % G, t),
+            )
+
+    def spread_group(w, j):
+        at_d = (d - j + G) % G
+        at = w * G + at_d
+        k = at * S + s
+
+        @pl.when(j > 0)
+        def _():
+            arrived(pg_all.at[k], pg_rsem.at[k])
+
+        for js in range(1, S):
+            send(
+                pg_all.at[k],
+                pg_all.at[k],
+                pgx_ssem.at[js, at],
+                pg_rsem.at[k],
+                ((s + js) % S, d, t),
+            )
+
+    def back_group(w, j):
+        at = w * G + (d - j + G) % G
+        for js in range(1, S):
+            k = at * S + (s + js) % S
+            arrived(pg_all.at[k], pg_rsem.at[k])
+        grad_part[...] = lax.dot_general(
+            pg_all[pl.ds(at * S, S)].reshape(S * rows, cols),
+            weight[...],
+            (((1,), (1,)), ((), ())),
+            preferred_element_type=F32,
+        ).reshape(S, Y, 2, piece, depth)
+        for at_y in range(Y):
+            keep[at, at_y] = grad_part[:, at_y, c]
+            core_send[at, at_y] = grad_part[:, at_y, 1 - c].astype(BF16)
+        send(core_send.at[at], core_recv.at[at], core_ssem.at[at], core_rsem.at[at], (s, d, mate))
+
+    def reduce_cores(w, j):
+        at = w * G + (d - j + G) % G
+        arrived(core_recv.at[at], core_rsem.at[at])
+        for dy in range(1, Y):
+            to_y = (y + dy) % Y
+            y_send[at, dy - 1] = (keep[at, to_y] + core_recv[at, to_y].astype(F32)).astype(BF16)
+            send(
+                y_send.at[at, dy - 1],
+                y_recv.at[at, Y - dy - 1],
+                y_ssem.at[at, dy - 1],
+                y_rsem.at[at, Y - dy - 1],
+                (s, d, to_y * 2 + c),
+            )
+        keep[at, y] = keep[at, y] + core_recv[at, y].astype(F32)
+
+    def finish_group(w, j):
+        at_d = (d - j + G) % G
+        at = w * G + at_d
+        total = keep[at, y]
+        for dy in range(1, Y):
+            arrived(y_recv.at[at, dy - 1], y_rsem.at[at, dy - 1])
+            total = total + y_recv[at, dy - 1].astype(F32)
+        last_send[at] = total.astype(BF16)
+        for js in range(S):
+            at_s = (s + js) % S
+
+            def push():
+                send(
+                    last_send.at[at, at_s],
+                    last_recv.at[me, w],
+                    last_ssem.at[at, at_s],
+                    last_rsem.at[me, w],
+                    (at_s, at_d, t),
+                )
+
+            if js > 0:
+                push()
+            else:
+                pl.when(j > 0)(push)
+
+    def back_tick(q):
+        stage(q, spread_group)
+        stage(q - 1, back_group)
+        stage(q - 2, reduce_cores)
+        stage(q - 3, finish_group)
+
+    loop(0, G + 3, forward_tick)
+    for js in range(1, S):
+        arrived(slots_all.at[js], slot_rsem.at[js])
+    finish_projection(0)
+    loop(G + 3, W * G + 3, forward_tick)
+    taken_first = placement(0)
+    finish_projection(1)
+    reply(0, taken_first)
+    taken_later = placement(1)
+    start_back(0)
+    reply(1, taken_later)
+    loop(0, 2, back_tick)
+    start_back(1)
+    loop(2, W * G + 3, back_tick)
+
+    for w in range(W):
+        last_recv[me, w] = last_send[w * G + d, s]
+
+    def collect(n):
+        @pl.when(n != me)
+        def _():
+            for w in range(W):
+                arrived(last_recv.at[n, w], last_rsem.at[n, w])
+
+    loop(0, N, collect)
+    plain = jnp.zeros((share, 1), F32)
+    crossed = jnp.zeros((share, 1), F32)
+    for n in range(N):
+        span = slice(n * depth, (n + 1) * depth)
+        weighted = last_recv[n].reshape(share, depth).astype(F32) * vision_gain[:, span]
+        plain = plain + jnp.sum(weighted, axis=1, keepdims=True)
+        crossed = crossed + jnp.sum(weighted * hat[n], axis=1, keepdims=True)
+    plain = plain / column_total
+    crossed = crossed / column_total
+    own_inv = inverse[:, 0:1]
+    for n in range(N):
+        span = slice(n * depth, (n + 1) * depth)
+        weighted = last_recv[n].reshape(share, depth).astype(F32) * vision_gain[:, span]
+        grad_out[:, span] = (own_inv * (weighted - plain - hat[n] * crossed)).astype(BF16)
+
+    def drain_block(k):
+        w, n = k // N, k % N
+
+        @pl.when(n != me)
+        def _():
+            arrived(x_in.at[n, w], x_ssem.at[k])
+
+        for i in range(2 * Y - 1):
+            arrived(x_all.at[k, t], fwd_ssem.at[i, k])
+
+    loop(0, W * N, drain_block)
+
+    def drain_group(at):
+        for js in range(1, S):
+            arrived(part_send.at[at, js - 1], part_ssem.at[js - 1, at])
+            arrived(pg_all.at[0], pgx_ssem.at[js, at])
+        arrived(core_send.at[at], core_ssem.at[at])
+        for dy in range(1, Y):
+            arrived(y_send.at[at, dy - 1], y_ssem.at[at, dy - 1])
+
+        @pl.when(at % G != d)
+        def _():
+            arrived(group_send.at[at], group_ssem.at[at])
+
+        for at_s in range(S):
+
+            @pl.when((at % G != d) | (s != at_s))
+            def _():
+                arrived(last_send.at[at, at_s], last_ssem.at[at, at_s])
+
+    loop(0, W * G, drain_group)
+    for js in range(1, S):
+        arrived(slots_row, slot_ssem.at[js])
+    for w in range(W):
+        for jd in range(1, G):
+            arrived(pg_all.at[0], pgz_ssem.at[w, jd])
+        for js in range(1, S):
+            arrived(features.at[w, 0], feat_ssem.at[w, js])
+            arrived(reply_send.at[w, js], reply_ssem.at[w, js])
+        for dt in range(1, T):
+            arrived(stats.at[w, 0], stat_ssem.at[w, dt])
+
+
+def exchange(
+    S, G, T, vision, vision_gain, vision_bias, weight, text, gain, slots, cotangent
+):
+    N, Y = S * G, T // 2
+    rows, column_total = vision.shape
+    share, depth = rows // T, weight.shape[0]
+    lang, cols = text.shape
+    W = WAVES
+    piece = share // W
+    part = piece * T
+    sem = pltpu.SemaphoreType.DMA
+    vmem = pltpu.VMEM
+    whole = pl.BlockSpec(memory_space=pltpu.VMEM)
+    return pl.pallas_call(
+        functools.partial(exchange_kernel, S, G, T),
+        out_shape=(
+            jax.ShapeDtypeStruct((lang, cols), BF16),
+            jax.ShapeDtypeStruct((share, column_total), BF16),
+        ),
+        in_specs=[pl.BlockSpec(memory_space=pl.ANY)] + [whole] * 7,
+        out_specs=(whole, whole),
+        scratch_shapes=[
+            vmem((share, column_total), BF16),
+            vmem((N, W, piece, depth), BF16),
+            vmem((N, share, depth), F32),
+            vmem((share, 128), F32),
+            vmem((8, part), jnp.int32),
+            vmem((W * N, T, piece, depth), BF16),
+            vmem((S, part, cols), F32),
+            vmem((W * G, part, cols), F32),
+            vmem((W * G, S - 1, part, cols), BF16),
+            vmem((S - 1, W * G, part, cols), BF16),
+            vmem((W * G, part, cols), BF16),
+            vmem((W, G - 1, part, cols), BF16),
+            vmem((W, part, cols), F32),
+            vmem((W, S, part, cols), BF16),
+            vmem((S, 8, part), jnp.int32),
+            vmem((W, lang, cols), F32),
+            vmem((W, T, 8, lang), F32),
+            vmem((W, S, part, cols), BF16),
+            vmem((W, S, part, cols), BF16),
+            vmem((W * N, part, cols), BF16),
+            vmem((S, Y, 2, piece, depth), F32),
+            vmem((W * G, Y, S, piece, depth), F32),
+            vmem((W * G, Y, S, piece, depth), BF16),
+            vmem((W * G, Y, S, piece, depth), BF16),
+            vmem((W * G, Y - 1, S, piece, depth), BF16),
+            vmem((W * G, Y - 1, S, piece, depth), BF16),
+            vmem((W * G, S, piece, depth), BF16),
+            vmem((N, W, piece, depth), BF16),
+            sem((W * N,)),
+            sem((W * N, T)),
+            sem((2 * Y - 1, W * N)),
+            sem((S - 1, W * G)),
+            sem((S - 1, W * G)),
+            sem((W * G,)),
+            sem((W, G - 1)),
+            sem((W, S)),
+            sem((W, S)),
+            sem((S,)),
+            sem((S,)),
+            sem((W, T)),
+            sem((W, T)),
+            sem((W, S)),
+            sem((W, S)),
+            sem((W, G)),
+            sem((S, W * G)),
+            sem((W * N,)),
+            sem((W * G,)),
+            sem((W * G,)),
+            sem((W * G, Y - 1)),
+            sem((W * G, Y - 1)),
+            sem((W * G, S)),
+            sem((N, W)),
+            sem,
+        ],
+        compiler_params=pltpu.CompilerParams(
+            collective_id=0, has_side_effects=True, vmem_limit_bytes=58 * 1024 * 1024
+        ),
+        cost_estimate=pl.CostEstimate(
+            flops=4 * N * rows * depth * cols, bytes_accessed=16 * 1024 * 1024, transcendentals=0
+        ),
+    )(
+        vision,
+        vision_gain[None, :],
+        vision_bias[None, :],
+        weight,
+        text,
+        gain[None, :],
+        slots.reshape(T, W, piece).transpose(1, 0, 2).reshape(W, part),
+        cotangent,
+    )
+
+
+def vision_backward(gathered, vision_gain, own_hat, own_inv):
+    normed_grad = gathered.transpose(1, 0, 2).reshape(own_hat.shape).astype(jnp.float32)
+    weighted = normed_grad * vision_gain
+    weighted_mean = jnp.mean(weighted, axis=1, keepdims=True)
+    vision_cross = jnp.mean(weighted * own_hat, axis=1, keepdims=True)
+    vision_grad = own_inv * (weighted - weighted_mean - own_hat * vision_cross)
+    return vision_grad.astype(jnp.bfloat16)
 
 
 def shards(
@@ -47,6 +676,27 @@
     column_total = vision_rows.shape[1]
     depth = proj_weight.shape[0]
     parts = sections * groups
+    if (
+        min(sections, groups) > 1
+        and parts <= 8
+        and tensor_count == 4
+        and row_total == 128
+        and lang_total == 128
+        and column_total % 128 == 0
+    ):
+        return exchange(
+            sections,
+            groups,
+            tensor_count,
+            vision_rows,
+            vision_gain,
+            vision_bias,
+            proj_weight,
+            text_rows,
+            text_gain,
+            slot_of_row,
+            out_cotangent,
+        )
     share = row_total // tensor_count
     share_start = lax.axis_index("tensor") * share
     own_rows = lax.dynamic_slice_in_dim(vision_rows, share_start, share, 0)
@@ -158,12 +808,7 @@
     gathered = lax.all_to_all(
         summed, ("section", "dp"), split_axis=0, concat_axis=0, tiled=True
     )
-    normed_grad = gathered.transpose(1, 0, 2).reshape(share, column_total).astype(jnp.float32)
-    weighted = normed_grad * vision_gain
-    weighted_mean = jnp.mean(weighted, axis=1, keepdims=True)
-    vision_cross = jnp.mean(weighted * own_hat, axis=1, keepdims=True)
-    vision_grad = own_inv * (weighted - weighted_mean - own_hat * vision_cross)
-    return (normed, vision_grad.astype(jnp.bfloat16))
+    return normed, vision_backward(gathered, vision_gain, own_hat, own_inv)
 
 
 def solution(mesh):

time: 361 us -> 129 us (0.36)
  waiting for transfers between devices: 200 us -> 0 us
  Pallas kernels: 0 us -> 120 us
  local copies, waits for them, and re-layouts: 48.5 us -> 8.09 us
  blocking collectives: 35.8 us -> 0 us
  other arithmetic: 31.5 us -> 0 us
  starting transfers between devices: 17.2 us -> 0 us
  between operations: 14 us -> 0.64 us
  matrix products: 12.6 us -> 0 us
    pallas_call x0 -> x1, Pallas kernels: none -> 120 us  [exchange(): pl.pallas_call(functools.partial(exchange_kernel, S, G, T), out_shape=(ja...]
    reduce_scatter x2 -> x0, waiting for transfers between devices: 93.4 us -> none  [the longest x1 55.1 us: shards(): lax.psum_scatter(partial_out.astype(jnp.bfloat16), ('section', 'dp'), sca...]
    all_gather x2 -> x0, waiting for transfers between devices: 76 us -> none  [the longest x1 47.9 us: shards(): lax.all_gather(projected_grad, ('section', 'dp'), axis=0, tiled=True)]
    all_to_all x4 -> x0, waiting for transfers between devices: 30.6 us -> none  [the longest x1 22.4 us: shards(): lax.all_to_all(summed, ('section', 'dp'), split_axis=0, concat_axis=0, ti...]
    all_to_all x1 -> x0, blocking collectives: 29.5 us -> none  [shards(): lax.all_to_all(outgoing, ('section', 'dp'), split_axis=0, concat_axis=0,...]
    all_to_all x4 -> x0, starting transfers between devices: 16.9 us -> none  [the longest x1 5.49 us: shards(): lax.all_to_all(summed, ('section', 'dp'), split_axis=0, concat_axis=0, ti...]
    dot_general x2 -> x0, matrix products: 12.6 us -> none  [the longest x1 7.22 us: shards(): jnp.dot(rows_all, proj_weight, preferred_element_type=jnp.float32)]
    convert_element_type x6 -> x0, other arithmetic: 11.9 us -> none  [the longest x1 2.57 us: shards(): return (normed, vision_grad.astype(jnp.bfloat16))]
  transfers between devices with their start and end apart: 8 -> 0, of which waited for: 8 -> 0; matrix products, arithmetic and copies ran while one was open for 3% -> 0% of each run, Pallas kernels for 0% -> 0%
where the time goes in v4:
time: 129 us
  Pallas kernels  120 us (93%)
  local copies, waits for them, and re-layouts  8.09 us (6%)
    pallas_call x1, Pallas kernels, exchange(): pl.pallas_call(functools.partial(exchange_kernel, S, G, T), out_shape=(ja...  120 us
    unnamed x2, local copies, waits for them, and re-layouts  3.76 us

profile of v4, /device:TPU:0, one launch (start us, length us, event | category | flops | bytes accessed | tf_op | source)
XLA Modules:
  0.0 128.8 jit_solution(5871671735430822076)
XLA Ops:
  0.6 0.7 reshape.10
  1.4 0.7 reshape.11.slots
  2.0 1.5 %broadcast_in_dim.9.vision_gain = f32[1,12800]{1,0:T(1,128)} reshape(f32[12800]{0:T(1024)} %param.9) | data formatting | bytes 102400 | tf_op jit(solution)/shard_map/broadcast_in_dim | solution.py:637
  3.5 1.5 %broadcast_in_dim.10.vision_bias = f32[1,12800]{1,0:T(1,128)} reshape(f32[12800]{0:T(1024)} %param.10) | data formatting | bytes 102400 | tf_op jit(solution)/shard_map/broadcast_in_dim | solution.py:638
  5.0 120.0 %shard_map.95 = (bf16[128,1024]{1,0:T(8,128)(2,1)}, bf16[32,12800]{1,0:T(8,128)(2,1)}) custom-call(bf16[128,12800]{1,0:T(8,128)(2,1)} %vision.1, f32[1,12800]{1,0:T(1,128)} %broadcast_in_dim.9.vision_gain, f32[1,12800]{1,0:T(1,128)} %broadcast_in_dim.10.vision_bias, bf16[1600,1024]{1,0:T(8,128)(2,1)} %weight.1, bf16[128,1024]{1,0:T(8,128)(2,1)} %text.1, ...), custom_call_target="tpu_custom_call" | custom-call | flops 6710886400 | bytes 16777216 | tf_op jit(solution)/shard_map/pallas_call | solution.py:566
  125.0 1.7 %copy.13 = bf16[128,1024]{1,0:T(8,128)(2,1)} copy(bf16[128,1024]{1,0:T(8,128)(2,1)} %get-tuple-element.4) | data formatting | bytes 524288
  126.7 2.1 %copy.14 = bf16[32,12800]{1,0:T(8,128)(2,1)} copy(bf16[32,12800]{1,0:T(8,128)(2,1)} %get-tuple-element.5) | data formatting | bytes 1638400
  (1 shorter events, 0.0 us)
